TPU v7x, 128 devices: a whole 4x4x4 slice. The times are simulated.
128 devices in a mesh: sec: 8 (over z, x_lo), tp: 16 (over x_hi, y, core).
Axes of the slice: x: 4 (x_hi: 2, x_lo: 2; x = x_hi * 2 + x_lo), y: 4, z: 4, core: 2. Of those that a mesh axis runs over, the one named last changes fastest.
Arguments:
- rollout: bfloat16 [16384, 8192], P('sec', 'tp'), may hold values from -96 to 96
- lengths: int32 [8, 8], P('sec'), may hold values from 1 to 256, as said below
- target: int32 [8, 8], P('sec'), may hold values from 0 to 7, as said below
- w_query: bfloat16 [8, 8192, 8192], P('sec', None, 'tp'), may hold values from -0.0625 to 0.0625
- w_keyval: bfloat16 [8, 8192, 2048], P('sec', None, 'tp'), may hold values from -0.0625 to 0.0625
- w_out: bfloat16 [8, 8192, 8192], P('sec', 'tp'), may hold values from -0.0625 to 0.0625
Outputs:
- attended: bfloat16 [8192, 8192], P('sec', 'tp')
Inputs may be any that keep to these rules, and one draw needn't show every extreme that they name: `lengths`: rollout group s holds its responses one after another from the first row of its block in the order of r; the rest of the block is not read. Every response holds at most 256 tokens and some response exactly 256. The responses that go to one section group hold at most 1024 tokens together, and some section group exactly 1024. `target`: every rollout group sends exactly one response to each section group.
All inputs are finite; a program needn't handle non-finite values.
Results may differ from a plain program's by a relative error of at most 0.012.
The roundings to bfloat16 on the way count: a program that leaves them out, or rounds other values in their place, can miss the bound.
Values may be sent and summed in bfloat16 or wider, within the bound.
No kernel may reach another device: no remote copies, remote signals or barrier semaphores. Data moves between devices by JAX's collectives and lax.ppermute only.
A program may use at most 128 MiB of HBM per device.

v0:
```python
import functools
import math

import jax
import jax.numpy as jnp
from jax import lax
from jax.experimental import pallas as pl
from jax.experimental.pallas import tpu as pltpu
from jax.sharding import PartitionSpec as P

HQ = 64
KVH = 8
HD = 128
CAP = 1024
SLOT = 256
ALIGN = 16
SENT = SLOT + ALIGN
TILE = 256
BLOCK = 512
rope_base = 500000.0
BF = jnp.bfloat16
F32 = jnp.float32


def params():
    return pltpu.CompilerParams(vmem_limit_bytes=14 << 20)


def permutation(move):
    pairs = []
    for t in range(16):
        x, y, c = move(t // 8, t // 2 % 4, t % 2)
        pairs.append((t, x % 2 * 8 + y % 4 * 2 + c % 2))
    return pairs


TO_CORE = permutation(lambda x, y, c: (x, y, c + 1))
TO_X = permutation(lambda x, y, c: (x + 1, y, c))
TO_Y = permutation(lambda x, y, c: (x, y + 1 - 2 * c, c))


def after(value, *others):
    return lax.optimization_barrier((value, *others))[0]


class Line:
    def __init__(self):
        self.last = None

    def next(self, value):
        return value if self.last is None else after(value, self.last)

    def add(self, result):
        self.last = jax.tree.leaves(result)[0]
        return result


def send(value, pairs):
    return lax.ppermute(value, "tp", pairs)


def in_hbm(array):
    return pltpu.with_memory_space_constraint(array, pltpu.HBM)


def cut_kernel(start_ref, rollout_ref, sent_ref):
    for d in range(8):
        row = pl.multiple_of(start_ref[d], ALIGN)
        sent_ref[d] = rollout_ref[pl.ds(row, SENT), :]


def cut(rollout, starts):
    return pl.pallas_call(
        cut_kernel,
        out_shape=jax.ShapeDtypeStruct((8, SENT, rollout.shape[1]), BF),
        in_specs=[
            pl.BlockSpec(memory_space=pltpu.SMEM),
            pl.BlockSpec(memory_space=pltpu.VMEM),
        ],
        out_specs=pl.BlockSpec(memory_space=pltpu.VMEM),
        compiler_params=params(),
        name="cut",
    )(starts, rollout)


def pack_kernel(plan_ref, arrived_ref, packed_ref, total_ref):
    first = pl.program_id(0) * TILE
    rows = first + lax.broadcasted_iota(jnp.int32, (TILE, 1), 0)
    slots = lax.broadcasted_iota(jnp.int32, (TILE, SENT), 1)
    total_ref[...] = jnp.zeros_like(total_ref)

    @pl.loop(0, 8)
    def _(s):
        begin, end = plan_ref[0, s], plan_ref[1, s]

        @pl.when((begin < first + TILE) & (end > first))
        def _():
            source = jnp.where(
                (rows >= begin) & (rows < end), rows + plan_ref[2, s], -1
            )
            picked = jnp.where(slots == source, 1.0, 0.0).astype(BF)
            total_ref[...] += jnp.dot(
                picked, arrived_ref[s], preferred_element_type=F32
            )

    packed_ref[...] = total_ref[...].astype(BF)


def pack(arrived, plan):
    width = arrived.shape[2]
    return pl.pallas_call(
        pack_kernel,
        out_shape=jax.ShapeDtypeStruct((CAP, width), BF),
        grid_spec=pltpu.PrefetchScalarGridSpec(
            num_scalar_prefetch=1,
            grid=(CAP // TILE,),
            in_specs=[pl.BlockSpec(memory_space=pltpu.VMEM)],
            out_specs=pl.BlockSpec((TILE, width), lambda i, p: (i, 0)),
            scratch_shapes=[pltpu.VMEM((TILE, width), F32)],
        ),
        compiler_params=params(),
        name="pack",
    )(plan, arrived)


def swap_members(values):
    lanes = lax.broadcasted_iota(jnp.int32, values.shape, 1)
    return jnp.where(
        lanes % 2 == 0, pltpu.roll(values, HD - 1, 1), pltpu.roll(values, 1, 1)
    )


def heads_first(keyval):
    to = lax.broadcasted_iota(jnp.int32, (HD, HD), 0)
    came = lax.broadcasted_iota(jnp.int32, (HD, HD), 1)
    order = jnp.where(came == to % 16 // 2 * 16 + to // 16 * 2 + to % 2, 1.0, 0.0).astype(BF)
    return lax.dot_general(
        order, keyval, (((1,), (1,)), ((), ())), preferred_element_type=F32
    ).astype(BF)


def project_kernel(counts, has_total, last, index_ref, *refs):
    refs = list(refs)
    pieces = [refs.pop(0) for _ in counts]
    query_w, keyval_w = refs.pop(0), refs.pop(0)
    total_ref = refs.pop(0) if has_total else None
    tables = [refs.pop(0) for _ in range(4)] if last else None
    weights_ref, sems = refs[-2:]
    refs = refs[:-2]
    columns = query_w.shape[1]
    depth = pieces[0].shape[2]
    copies = []
    for k in range(sum(counts)):
        rows = pl.ds(pl.multiple_of(index_ref[k] * depth, depth), depth)
        copies.append((
            pltpu.make_async_copy(
                query_w.at[rows, :], weights_ref.at[k, :, pl.ds(0, columns)], sems.at[k, 0]
            ),
            pltpu.make_async_copy(
                keyval_w.at[rows, :], weights_ref.at[k, :, pl.ds(columns, HD)], sems.at[k, 1]
            ),
        ))

    @pl.when(pl.program_id(0) == 0)
    def _():
        for pair in copies:
            for copy in pair:
                copy.start()

    query = total_ref[:, :columns] if has_total else 0.0
    keyval = total_ref[:, columns:] if has_total else 0.0
    k = 0
    for ref, count in zip(pieces, counts):
        for j in range(count):

            @pl.when(pl.program_id(0) == 0)
            def _(k=k):
                for copy in copies[k]:
                    copy.wait()

            left = ref[j]
            query += jnp.dot(left, weights_ref[k, :, :columns], preferred_element_type=F32)
            keyval += jnp.dot(left, weights_ref[k, :, columns:], preferred_element_type=F32)
            k += 1
    if not last:
        refs[0][:, :columns] = query
        refs[0][:, columns:] = keyval
        return
    query_out, keyval_out = refs
    q_cos, q_sin, kv_cos, kv_sin = [t[...] for t in tables]
    for head in range(columns // HD):
        span = slice(head * HD, (head + 1) * HD)
        part = query[:, span]
        query_out[:, span] = (part * q_cos + swap_members(part) * q_sin).astype(BF)
    turned = (keyval * kv_cos + swap_members(keyval) * kv_sin).astype(BF)
    turned = heads_first(turned)
    for member in range(2 * KVH):
        keyval_out[member] = turned[member // 2 * 16 : member // 2 * 16 + 16]


def project(pieces, index, w_query, w_keyval, rows, total=None, tables=None, block=0):
    counts = tuple(p.shape[0] for p in pieces)
    n = sum(counts)
    width = pieces[0].shape[2]
    columns = w_query.shape[1]
    last = tables is not None

    def skip(array, axis):
        return block * (BLOCK // TILE) if array.shape[axis] > rows else 0

    in_specs = [
        pl.BlockSpec((p.shape[0], TILE, width), lambda i, _, at=skip(p, 1): (0, i + at, 0))
        for p in pieces
    ]
    in_specs += [pl.BlockSpec(memory_space=pltpu.HBM)] * 2
    operands = list(pieces) + [in_hbm(w_query), in_hbm(w_keyval)]
    if total is not None:
        at = skip(total, 0)
        in_specs.append(pl.BlockSpec((TILE, columns + HD), lambda i, _: (i + at, 0)))
        operands.append(in_hbm(total))
    if last:
        first = skip(tables[0], 0)
        in_specs += [pl.BlockSpec((TILE, HD), lambda i, _: (i + first, 0))] * 4
        operands += [in_hbm(t) for t in tables]
        out_shape = (
            jax.ShapeDtypeStruct((rows, columns), BF),
            jax.ShapeDtypeStruct((2 * KVH, 16, rows), BF),
        )
        out_specs = [
            pl.BlockSpec((TILE, columns), lambda i, _: (i, 0)),
            pl.BlockSpec((2 * KVH, 16, TILE), lambda i, _: (0, 0, i)),
        ]
    else:
        out_shape = jax.ShapeDtypeStruct((rows, columns + HD), F32)
        out_specs = pl.BlockSpec((TILE, columns + HD), lambda i, _: (i, 0))
    return pl.pallas_call(
        functools.partial(project_kernel, counts, total is not None, last),
        out_shape=out_shape,
        grid_spec=pltpu.PrefetchScalarGridSpec(
            num_scalar_prefetch=1,
            grid=(rows // TILE,),
            in_specs=in_specs,
            out_specs=out_specs,
            scratch_shapes=[
                pltpu.VMEM((n, width, columns + HD), BF),
                pltpu.SemaphoreType.DMA((n, 2)),
            ],
        ),
        compiler_params=params(),
        name="project",
    )(index, *operands)


def project_block_kernel(skips, last, index_ref, *refs):
    refs = list(refs)
    n = len(skips) - 2
    pieces = [refs.pop(0) for _ in range(n)]
    query_w, keyval_w, total = refs.pop(0), refs.pop(0), refs.pop(0)
    tables = [refs.pop(0) for _ in range(4)] if last else []
    *outs, left_ref, weights_ref, sum_ref, table_ref, sems = refs
    depth, columns = left_ref.shape[2], query_w.shape[1]
    copy = pltpu.make_async_copy
    fetches = []
    for k, piece in enumerate(pieces):
        rows = pl.ds(pl.multiple_of(index_ref[k] * depth, depth), depth)
        fetches.append([
            copy(piece.at[pl.ds(skips[k], BLOCK), :], left_ref.at[k], sems.at[k, 0]),
            copy(query_w.at[rows, :], weights_ref.at[k, :, pl.ds(0, columns)], sems.at[k, 1]),
            copy(keyval_w.at[rows, :], weights_ref.at[k, :, pl.ds(columns, HD)], sems.at[k, 2]),
        ])
    fetch_total = copy(total.at[pl.ds(skips[n], BLOCK), :], sum_ref, sems.at[n, 0])
    fetch_tables = [
        copy(table.at[pl.ds(skips[n + 1], BLOCK), :], table_ref.at[j], sems.at[n + 1, j])
        for j, table in enumerate(tables)
    ]
    for fetch in [*fetches[0], fetch_total, *sum(fetches[1:], []), *fetch_tables]:
        fetch.start()
    for k in range(n):
        for fetch in fetches[k]:
            fetch.wait()
        if k == 0:
            fetch_total.wait()
        for tile in range(BLOCK // TILE):
            rows = slice(tile * TILE, (tile + 1) * TILE)
            left = left_ref[k, rows, :]
            for span in (slice(0, columns), slice(columns, columns + HD)):
                sum_ref[rows, span] += jnp.dot(
                    left, weights_ref[k, :, span], preferred_element_type=F32
                )
    for fetch in fetch_tables:
        fetch.wait()
    if not last:
        outs[0][...] = sum_ref[...]
        return
    query_out, keyval_out = outs
    for tile in range(BLOCK // TILE):
        rows = slice(tile * TILE, (tile + 1) * TILE)
        q_cos, q_sin, kv_cos, kv_sin = [table_ref[j, rows, :] for j in range(4)]
        for head in range(columns // HD):
            span = slice(head * HD, (head + 1) * HD)
            part = sum_ref[rows, span]
            query_out[rows, span] = (part * q_cos + swap_members(part) * q_sin).astype(BF)
        part = sum_ref[rows, columns:]
        turned = heads_first((part * kv_cos + swap_members(part) * kv_sin).astype(BF))
        for member in range(2 * KVH):
            keyval_out[member, :, rows] = turned[member // 2 * 16 : member // 2 * 16 + 16]


def project_block(pieces, index, w_query, w_keyval, block, total, tables=()):
    n = len(pieces)
    width, columns = pieces[0].shape[1], w_query.shape[1]
    last = len(tables) > 0
    skips = [
        block * BLOCK if a.shape[0] > BLOCK else 0 for a in (*pieces, total, *tables[:1])
    ]
    if not last:
        skips.append(0)
    operands = [in_hbm(a) for a in (*pieces, w_query, w_keyval, total, *tables)]
    if last:
        out_shape = (
            jax.ShapeDtypeStruct((BLOCK, columns), BF),
            jax.ShapeDtypeStruct((2 * KVH, 16, BLOCK), BF),
        )
    else:
        out_shape = (jax.ShapeDtypeStruct((BLOCK, columns + HD), F32),)
    return pl.pallas_call(
        functools.partial(project_block_kernel, tuple(skips), last),
        out_shape=out_shape,
        in_specs=[pl.BlockSpec(memory_space=pltpu.SMEM)]
        + [pl.BlockSpec(memory_space=pltpu.HBM)] * len(operands),
        out_specs=[pl.BlockSpec(memory_space=pltpu.VMEM)] * len(out_shape),
        scratch_shapes=[
            pltpu.VMEM((n, BLOCK, width), BF),
            pltpu.VMEM((n, width, columns + HD), BF),
            pltpu.VMEM((BLOCK, columns + HD), F32),
            pltpu.VMEM((4, BLOCK, HD), F32),
            pltpu.SemaphoreType.DMA((n + 2, 4)),
        ],
        compiler_params=params(),
        name="project_block",
    )(index, *operands)


def attend_kernel(block, plan_ref, query_ref, *refs):
    keyval_refs, heads_ref = refs[:-1], refs[-1]
    scale = 1.0 / math.sqrt(HD)
    local_heads = query_ref.shape[1] // HD

    def columns_of(there, member):
        part, first = there * TILE // BLOCK, there * TILE % BLOCK
        return keyval_refs[part][member * HD : (member + 1) * HD, first : first + TILE]

    for tile in range(BLOCK // TILE):
        here = block * (BLOCK // TILE) + tile
        rows = here * TILE + lax.broadcasted_iota(jnp.int32, (TILE, 1), 0)
        begin = jnp.zeros((TILE, 1), jnp.int32)
        for s in range(8):
            begin = jnp.where(rows >= plan_ref[0, s], plan_ref[0, s], begin)
        filled = rows < plan_ref[1, 7]
        seen = []
        for there in range(max(here - 1, 0), here + 1):
            columns = there * TILE + lax.broadcasted_iota(jnp.int32, (TILE, TILE), 1)
            allowed = (columns >= begin) & (columns <= rows)
            seen.append((allowed, columns_of(there, 0), columns_of(there, 1)))
        for head in range(local_heads):
            span = slice(head * HD, (head + 1) * HD)
            query = query_ref[tile * TILE : (tile + 1) * TILE, span]
            scores = []
            for allowed, key, _ in seen:
                raw = jnp.dot(query, key, preferred_element_type=F32)
                scores.append(jnp.where(allowed, raw * scale, -1e30))
            top = functools.reduce(
                jnp.maximum, [jnp.max(s, axis=1, keepdims=True) for s in scores]
            )
            shifted = [jnp.exp(s - top) for s in scores]
            norm = sum(jnp.sum(s, axis=1, keepdims=True) for s in shifted)
            result = jnp.zeros((TILE, HD), F32)
            for part, (_, _, value) in zip(shifted, seen):
                weights = (part / norm).astype(BF)
                result += lax.dot_general(
                    weights, value, (((1,), (1,)), ((), ())), preferred_element_type=F32
                )
            heads_ref[tile * TILE : (tile + 1) * TILE, span] = jnp.where(
                filled, result, 0.0
            ).astype(BF)


def attend(block, plan, query, keyvals):
    return pl.pallas_call(
        functools.partial(attend_kernel, block),
        out_shape=jax.ShapeDtypeStruct(query.shape, BF),
        in_specs=[
            pl.BlockSpec(memory_space=pltpu.SMEM),
            pl.BlockSpec(memory_space=pltpu.VMEM),
        ]
        + [pl.BlockSpec(memory_space=pltpu.VMEM)] * len(keyvals),
        out_specs=pl.BlockSpec(memory_space=pltpu.VMEM),
        compiler_params=params(),
        name="attend",
    )(plan, query, *keyvals)


def chunks_kernel(groups, adds, index_ref, heads_ref, w_out, *refs):
    n = len(adds)
    refs = list(refs)
    weights_ref, sems = refs[-2:]
    outs = refs[-2 - len(groups) : -2]
    width = weights_ref.shape[2]
    copies = []
    for k in range(n):
        columns = pl.ds(pl.multiple_of(index_ref[k] * width, width), width)
        copies.append(
            pltpu.make_async_copy(w_out.at[:, columns], weights_ref.at[k], sems.at[k])
        )

    @pl.when(pl.program_id(0) == 0)
    def _():
        for copy in copies:
            copy.start()

    k = 0
    for out, size in zip(outs, groups):
        for j in range(size):

            @pl.when(pl.program_id(0) == 0)
            def _(k=k):
                copies[k].wait()

            total = jnp.dot(heads_ref[...], weights_ref[k], preferred_element_type=F32)
            for _ in range(adds[k]):
                total += refs.pop(0)[0].astype(F32)
            out[j] = total.astype(BF)
            k += 1


def chunks(heads, w_out, index, groups, adds, block=None, into=None):
    rows, depth = heads.shape
    width = 512
    n = len(adds)
    in_specs = [
        pl.BlockSpec((TILE, depth), lambda i, p: (i, 0)),
        pl.BlockSpec(memory_space=pltpu.HBM),
    ]
    operands = [heads, in_hbm(w_out)]
    for terms in adds:
        for array, place in terms:
            in_specs.append(
                pl.BlockSpec((1, TILE, width), lambda i, p, at=place: (at, i, 0))
            )
            operands.append(array)
    first = 0 if block is None else block * (BLOCK // TILE)
    out_rows = rows if block is None else CAP
    aliases = {}
    if into is not None:
        in_specs.append(pl.BlockSpec(memory_space=pl.ANY))
        operands.append(into)
        aliases = {len(operands): 0}
    return pl.pallas_call(
        functools.partial(chunks_kernel, groups, tuple(len(a) for a in adds)),
        input_output_aliases=aliases,
        out_shape=[jax.ShapeDtypeStruct((g, out_rows, width), BF) for g in groups],
        grid_spec=pltpu.PrefetchScalarGridSpec(
            num_scalar_prefetch=1,
            grid=(rows // TILE,),
            in_specs=in_specs,
            out_specs=[
                pl.BlockSpec((g, TILE, width), lambda i, p: (0, i + first, 0)) for g in groups
            ],
            scratch_shapes=[
                pltpu.VMEM((n, depth, width), BF),
                pltpu.SemaphoreType.DMA((n,)),
            ],
        ),
        compiler_params=params(),
        name="chunks",
    )(index, *operands)


def gather_order(x, y, c):
    way = 1 - 2 * c
    places = [(x, y, c), (x, y, 1 - c), (x, y - way, c), (x, y - way, 1 - c)]
    places += [(x, y + way, 1 - c), (x, y + way, c)]
    places += [(1 - x, y, c), (1 - x, y, 1 - c), (x, y + 2, c), (x, y + 2, 1 - c)]
    places += [(1 - x, y - way, c), (1 - x, y - way, 1 - c)]
    places += [(1 - x, y + way, 1 - c), (1 - x, y + way, c)]
    places += [(1 - x, y + 2, c), (1 - x, y + 2, 1 - c)]
    return jnp.stack(
        [side * 8 + (row + 4) % 4 * 2 + core for side, row, core in places]
    ).astype(jnp.int32)


def rotary_tables(position, member):
    lanes = jnp.arange(HD, dtype=jnp.int32)
    sign = jnp.where(lanes % 2 == 0, -1.0, 1.0).astype(F32)

    def table(pairs):
        frequency = jnp.exp(pairs.astype(F32) * (-2.0 * math.log(rope_base) / HD))
        angles = position.astype(F32)[:, None] * frequency[None, :]
        return jnp.cos(angles), jnp.sin(angles) * sign[None, :]

    q_cos, q_sin = table(lanes // 2)
    columns = member * HD + lanes
    kv_cos, kv_sin = table(columns // (2 * KVH) % (HD // 2))
    keys = member < KVH
    return q_cos, q_sin, jnp.where(keys, kv_cos, 1.0), jnp.where(keys, kv_sin, 0.0)


def body(rollout, lengths, target, w_query, w_keyval, w_out):
    member = lax.axis_index("tp")
    x, y, c = member // 8, member // 2 % 4, member % 2
    section_ids = jnp.arange(8, dtype=jnp.int32)
    own_lengths = lengths[0]
    chosen = target[0][None, :] == section_ids[:, None]
    before = jnp.cumsum(own_lengths) - own_lengths
    start_to = jnp.sum(jnp.where(chosen, before[None, :], 0), axis=1)
    sent_from = jnp.minimum(start_to // ALIGN * ALIGN, rollout.shape[0] - SENT)
    count_to = jnp.sum(jnp.where(chosen, own_lengths[None, :], 0), axis=1)
    facts = jnp.stack([count_to, start_to - sent_from], axis=1)
    outgoing = cut(rollout, sent_from)
    arrived = lax.all_to_all(outgoing, "sec", split_axis=0, concat_axis=0, tiled=True)
    facts = lax.all_to_all(facts, "sec", split_axis=0, concat_axis=0, tiled=True)
    counts, shifts = facts[:, 0], facts[:, 1]
    ends = jnp.cumsum(counts)
    offsets = ends - counts
    plan = jnp.stack([offsets, ends, shifts - offsets])
    row_ids = jnp.arange(CAP, dtype=jnp.int32)
    begin = jnp.max(
        jnp.where(row_ids[:, None] >= offsets[None, :], offsets[None, :], 0), axis=1
    )
    order = gather_order(x, y, c)
    weights = w_query[0], w_keyval[0]
    w_out = w_out[0]
    line = Line()
    way = 1 - 2 * c
    sides = (1 - x, x)

    def at(*places):
        return jnp.stack(
            [side * 8 + (row + 4) % 4 * 2 + core for side, row, core in places]
        ).astype(jnp.int32)

    def move(value, pairs):
        return send(line.next(value), pairs)

    def stack(*arrays):
        return line.add(jnp.stack([line.next(arrays[0]), *arrays[1:]]))

    def part(value, *index):
        return line.add(line.next(value)[index])

    def projected(pieces, index, *more):
        pieces = [p[None] for p in pieces]
        return line.add(project(pieces, line.next(index), *weights, *more))

    def projected_block(pieces, index, *more):
        return line.add(project_block(pieces, line.next(index), *weights, *more))

    def spread(keyval):
        keyval = lax.all_to_all(
            line.next(keyval), "tp", split_axis=0, concat_axis=0, tiled=True
        )
        return keyval.reshape(2 * HD, BLOCK)

    def attended(block, query, keyvals):
        return line.add(attend(block, line.next(plan), query, keyvals))

    def join(*arrays):
        *arrays, line.last = lax.optimization_barrier((*arrays, line.last))
        return arrays

    def summed(heads, places, groups, adds, **where):
        index = line.next(at(*places))
        return line.add(chunks(heads, w_out, index, groups, adds, **where))

    def for_core(heads, places):
        parts = summed(heads, places, (1,) * len(places), [[]] * len(places))
        return [send(p, TO_CORE) for p in parts]

    def far_for_core(heads):
        return for_core(heads, [(side, y + 2, 1 - c) for side in sides])

    def near_for_core(heads):
        places = []
        for side in sides:
            places += [(side, y - way, 1 - c), (side, y - way, c)]
        return for_core(heads, places)

    def far_sums(heads, passed):
        places = [(side, y + 2, c) for side in sides]
        adds = [[(p, 0)] for p in passed]
        return send(summed(heads, places, (2,), adds)[0], TO_Y)

    def near_sums(heads, passed, far, groups):
        places, adds = [], []
        for i, side in enumerate(sides):
            places += [(side, y + way, c), (side, y + way, 1 - c)]
            adds += [[(passed[2 * i], 0), (far, i)], [(passed[2 * i + 1], 0)]]
        return summed(heads, places, groups, adds)

    def last_sum(i, heads, near, *more, wait=None, **where):
        shared = summed(heads, [(sides[i], y, 1 - c)], (1,), [[(near, 1)]])[0]
        if wait is not None:
            near = after(near, wait)
        terms = [(t, 0) for t in (near, send(shared, TO_CORE), *more)]
        return summed(heads, [(sides[i], y, c)], (1,), [terms], **where)[0]


    value = line.add(pack(arrived, plan))
    across = send(value, TO_X)
    up = send(value, TO_Y)
    other = send(value, TO_CORE)
    up_other = send(other, TO_Y)
    position = line.next(row_ids) - begin
    tables = line.add(rotary_tables(position, member))
    total = projected([value, other, up], order[:3], CAP)
    across, up_other = join(across, up_other)
    there_up1 = [send(u[BLOCK:], TO_X) for u in (up, up_other)]
    far = send(up, TO_Y)
    across_other = send(across, TO_CORE)
    there_up0 = [send(a[:BLOCK], TO_Y) for a in (across, across_other)]
    down, down_other = send(up, TO_CORE), send(up_other, TO_CORE)
    pieces = [up_other, down, down_other, across, across_other]
    total = projected(pieces, order[3:8], CAP, total)
    far_high = after(far, total)[BLOCK:]
    far, far_high, *there_up = join(far, far_high, *there_up0, *there_up1)
    there_far0 = send(there_up[0], TO_Y)
    there_far1 = send(far_high, TO_X)
    far_other = send(far, TO_CORE)
    there_down = [send(u, TO_CORE) for u in there_up]
    pieces = [far, far_other, *there_up[:2], *there_down[:2]]
    total0 = projected_block(pieces, order[8:14], 0, total)[0]
    there_far0, far = join(there_far0, far)
    pieces = [there_far0, send(there_far0, TO_CORE)]
    index = after(order[14:], there_far1)
    query0, keyval0 = projected_block(pieces, index, 0, total0, tables)
    keyval0 = spread(keyval0)
    pieces = [far, far_other, *there_up[2:], *there_down[2:]]
    pieces += [there_far1, move(there_far1, TO_CORE)]
    query1, keyval1 = projected_block(pieces, order[8:], 1, total, tables)
    keyval1 = spread(keyval1)

    heads0 = attended(0, query0, [keyval0])
    far0 = far_sums(heads0, far_for_core(heads0))
    heads1 = attended(1, query1, [keyval0, keyval1])
    far1 = far_sums(heads1, far_for_core(heads1))
    passed = near_for_core(heads0)
    near0 = [send(t, TO_Y) for t in near_sums(heads0, passed, far0, (2, 2))]
    passed = near_for_core(heads1)
    near1 = [send(t, TO_Y) for t in near_sums(heads1, passed, far1, (2, 2))]
    crossed0 = send(last_sum(0, heads0, near0[0]), TO_X)
    crossed1 = send(last_sum(0, heads1, near1[0], wait=crossed0), TO_X)
    result = last_sum(1, heads0, near0[1], crossed0, block=0)
    return last_sum(1, heads1, near1[1], crossed1, block=1, into=result)[0]


def solution(mesh):
    placed = (
        P("sec", "tp"),
        P("sec", None),
        P("sec", None),
        P("sec", None, "tp"),
        P("sec", None, "tp"),
        P("sec", "tp", None),
    )
    return jax.shard_map(
        body, mesh=mesh, in_specs=placed, out_specs=P("sec", "tp"), check_vma=False
    )
```

profile of v0, /device:TPU:1, one launch (start us, length us, event | category | flops | bytes accessed | tf_op | source)
XLA Modules:
  0.0 263.2 jit_solution(7407122255792398506)
XLA Ops:
  3.0 6.8 %all-to-all-start = ((s32[8,1,2]{2,1,0:T(1,128)}), s32[8,1,2]{2,1,0:T(1,128)S(1)}, u32[]{:S(2)}, u32[]{:S(2)}) async-start(s32[8,1,2]{2,1,0:T(1,128)} %copy.10), calls=%async_computation | async-start | bytes 8192 | tf_op jit(solution)/shard_map/all_to_all | solution.py:521
  11.4 2.0 cut.1
  14.7 3.9 %all-to-all-start.1 = ((bf16[8,272,512]{2,1,0:T(8,128)(2,1)}), bf16[8,272,512]{2,1,0:T(8,128)(2,1)S(1)}, u32[]{:S(2)}, u32[]{:S(2)}) async-start(bf16[8,272,512]{2,1,0:T(8,128)(2,1)} %cut.1), calls=%async_computation.1 | async-start | bytes 4456448 | tf_op jit(solution)/shard_map/all_to_all | solution.py:520
  18.9 26.3 %all-to-all-done.1.arrived_ref = bf16[8,272,512]{2,1,0:T(8,128)(2,1)S(1)} async-done(((bf16[8,272,512]{2,1,0:T(8,128)(2,1)}), bf16[8,272,512]{2,1,0:T(8,128)(2,1)S(1)}, u32[]{:S(2)}, u32[]{:S(2)}) %all-to-all-start.1) | async-done | bytes 2228256 | tf_op jit(solution)/shard_map/all_to_all | solution.py:520
  45.2 4.0 %pack.1 = bf16[1024,512]{1,0:T(8,128)(2,1)S(1)} custom-call(s32[3,8]{1,0:T(4,128)S(1)} %pad_add_fusion.plan_ref, bf16[8,272,512]{2,1,0:T(8,128)(2,1)S(1)} %all-to-all-done.1.arrived_ref), custom_call_target="tpu_custom_call" | custom-call | tf_op jit(solution)/shard_map/pack/pallas_call | solution.py:111
  49.3 2.8 %collective-permute-start.3 = (bf16[1024,512]{1,0:T(8,128)(2,1)S(1)}, bf16[1024,512]{1,0:T(8,128)(2,1)}, u32[]{:S(2)}, u32[]{:S(2)}) collective-permute-start(bf16[1024,512]{1,0:T(8,128)(2,1)S(1)} %pack.1), channel_id=1, source_target_pairs={{0,1},{1,0},{2,3},{3,2},{4,5},{5,4},{6,7},{7,6},{8,9},{9,8},{10,11... | collective-permute-start | bytes 3145736 | tf_op jit(solution)/shard_map/ppermute | solution.py:59
  52.1 2.8 %collective-permute-start = (bf16[1024,512]{1,0:T(8,128)(2,1)S(1)}, bf16[1024,512]{1,0:T(8,128)(2,1)S(1)}, u32[]{:S(2)}, u32[]{:S(2)}) collective-permute-start(bf16[1024,512]{1,0:T(8,128)(2,1)S(1)} %pack.1), channel_id=1, source_target_pairs={{0,2},{1,7},{2,4},{3,1},{4,6},{5,3},{6,0},{7,5},{8,10},{9,15},{10,... | collective-permute-start | bytes 3145736 | tf_op jit(solution)/shard_map/ppermute | solution.py:59
  54.9 2.4 collective-permute-start.2
  58.0 5.5 %fusion.3 = (f32[1024,128]{1,0:T(8,128)}, f32[1024,128]{1,0:T(8,128)}, f32[1024,128]{1,0:T(8,128)}, f32[1024,128]{1,0:T(8,128)}) fusion(f32[128]{0:T(128)S(1)} %fusion.9, f32[128]{0:T(128)S(1)} %get-tuple-element.127, f32[1024]{0:T(1024)S(1)} %subtract_convert_fusion, pred[]{:T(512)S(6)} %lt.136, f32[128]{0:T(128)S(1)} %get-tuple-element.128), kind=kLoop, calls=%fused_computation.7 | loop fusion | flops 786432 | bytes 2102785 | tf_op jit(solution)/shard_map/jit(_where)/select_n | solution.py:505
  63.5 3.2 %collective-permute-done = bf16[1024,512]{1,0:T(8,128)(2,1)S(1)} collective-permute-done((bf16[1024,512]{1,0:T(8,128)(2,1)S(1)}, bf16[1024,512]{1,0:T(8,128)(2,1)S(1)}, u32[]{:S(2)}, u32[]{:S(2)}) %collective-permute-start) | collective-permute-done | bytes 1048608 | tf_op jit(solution)/shard_map/ppermute | solution.py:59
  66.7 6.9 %project.2.refs_7_ = f32[1024,640]{1,0:T(8,128)S(1)} custom-call(s32[3]{0:T(128)S(1)} %pad_add_fusion.6.index_ref, bf16[1,1024,512]{2,1,0:T(8,128)(2,1)S(1)} %bitcast.59, bf16[1,1024,512]{2,1,0:T(8,128)(2,1)} %bitcast.28.refs_1_, bf16[1,1024,512]{2,1,0:T(8,128)(2,1)S(1)} %bitcast.60, bf16[8192,512]{1,0:T(8,128)(2,1)} %bitcast.85, bf16[8192,128]{1,0:T(8,128)(2,1)} %bitcast.90), custom_call_target="tpu_custom_call" | custom-call | tf_op jit(solution)/shard_map/project/pallas_call | solution.py:236
  75.1 5.7 %collective-permute-done.2 = bf16[1024,512]{1,0:T(8,128)(2,1)S(1)} collective-permute-done((bf16[1024,512]{1,0:T(8,128)(2,1)S(1)}, bf16[1024,512]{1,0:T(8,128)(2,1)S(1)}, u32[]{:S(2)}, u32[]{:S(2)}) %collective-permute-start.2) | collective-permute-done | bytes 1048608 | tf_op jit(solution)/shard_map/ppermute | solution.py:59
  83.8 2.4 collective-permute-start.10
  95.4 10.6 %project.3.refs_8_.refs_10_ = f32[1024,640]{1,0:T(8,128)S(1)} custom-call(s32[5]{0:T(128)S(1)} %stack.145.index_ref, bf16[1,1024,512]{2,1,0:T(8,128)(2,1)S(1)} %bitcast.62, bf16[1,1024,512]{2,1,0:T(8,128)(2,1)S(1)} %bitcast.66, bf16[1,1024,512]{2,1,0:T(8,128)(2,1)S(1)} %bitcast.67, bf16[1,1024,512]{2,1,0:T(8,128)(2,1)S(1)} %bitcast.61, ...), custom_call_target="tpu_custom_call" | custom-call | tf_op jit(solution)/shard_map/project/pallas_call | solution.py:236
  107.5 1.9 slice.33
  109.7 1.7 collective-permute-start.14
  113.5 2.5 collective-permute-start.12
  116.9 6.0 %project_block.3.refs_4_ = f32[512,640]{1,0:T(8,128)S(1)} custom-call(s32[6]{0:T(128)S(1)} %stack.147.index_ref, bf16[1024,512]{1,0:T(8,128)(2,1)} %collective-permute-done.1.refs_0_, bf16[1024,512]{1,0:T(8,128)(2,1)} %copy-done.12, bf16[512,512]{1,0:T(8,128)(2,1)} %collective-permute-done.8.refs_2_, bf16[512,512]{1,0:T(8,128)(2,1)} %collective-permute-done.9.refs_3_, ...), custom_call_target="tpu_custom_call" | custom-call | tf_op jit(solution)/shard_map/project_block/pallas_call | solution.py:326
  125.2 3.1 %collective-permute-done.12.refs_6_ = bf16[512,512]{1,0:T(8,128)(2,1)S(1)} collective-permute-done((bf16[512,512]{1,0:T(8,128)(2,1)}, bf16[512,512]{1,0:T(8,128)(2,1)S(1)}, u32[]{:S(2)}, u32[]{:S(2)}) %collective-permute-start.12) | collective-permute-done | bytes 524320 | tf_op jit(solution)/shard_map/ppermute | solution.py:59
  129.2 5.0 %project_block.4 = (bf16[512,512]{1,0:T(8,128)(2,1)S(1)}, bf16[16,16,512]{2,1,0:T(8,128)(2,1)}) custom-call(s32[2]{0:T(128)S(1)} %pad_add_fusion.5.index_ref, bf16[512,512]{1,0:T(8,128)(2,1)} %copy-done.13, bf16[512,512]{1,0:T(8,128)(2,1)} %collective-permute-done.17.refs_1_, bf16[8192,512]{1,0:T(8,128)(2,1)} %bitcast.88, bf16[8192,128]{1,0:T(8,128)(2,1)} %bitcast.93, ...), custom_call_target="tpu_custom_call" | custom-call | tf_op jit(solution)/shard_map/project_block/pallas_call | solution.py:326
  135.4 5.6 %all-to-all-start.2 = ((bf16[16,16,512]{2,1,0:T(8,128)(2,1)}), bf16[16,16,512]{2,1,0:T(8,128)(2,1)S(1)}, u32[]{:S(2)}, u32[]{:S(2)}) async-start(bf16[16,16,512]{2,1,0:T(8,128)(2,1)} %get-tuple-element.82), calls=%async_computation.2 | async-start | bytes 524288 | tf_op jit(solution)/shard_map/all_to_all | solution.py:559
  143.0 8.7 %project_block.5 = (bf16[512,512]{1,0:T(8,128)(2,1)S(1)}, bf16[16,16,512]{2,1,0:T(8,128)(2,1)}) custom-call(s32[8]{0:T(128)S(1)} %stack.143.index_ref, bf16[1024,512]{1,0:T(8,128)(2,1)} %collective-permute-done.1.refs_0_, bf16[1024,512]{1,0:T(8,128)(2,1)} %copy-done.12, bf16[512,512]{1,0:T(8,128)(2,1)} %collective-permute-done.10.refs_2_, ...), custom_call_target="tpu_custom_call" | custom-call | tf_op jit(solution)/shard_map/project_block/pallas_call | solution.py:326
  152.5 2.6 attend.2.heads_ref
  155.1 2.8 %chunks.16 = (bf16[1,512,512]{2,1,0:T(8,128)(2,1)S(1)}, bf16[1,512,512]{2,1,0:T(8,128)(2,1)S(1)}) custom-call(s32[2]{0:T(128)S(1)} %pad_add_fusion.4.index_ref, bf16[512,512]{1,0:T(8,128)(2,1)S(1)} %attend.2.heads_ref, bf16[512,8192]{1,0:T(8,128)(2,1)} %bitcast.69), custom_call_target="tpu_custom_call" | custom-call | tf_op jit(solution)/shard_map/chunks/pallas_call | solution.py:458
  158.5 7.2 %all-to-all-start.3 = ((bf16[16,16,512]{2,1,0:T(8,128)(2,1)}), bf16[16,16,512]{2,1,0:T(8,128)(2,1)S(1)}, u32[]{:S(2)}, u32[]{:S(2)}) async-start(bf16[16,16,512]{2,1,0:T(8,128)(2,1)} %get-tuple-element.89), calls=%async_computation.3 | async-start | bytes 524288 | tf_op jit(solution)/shard_map/all_to_all | solution.py:559
  165.9 2.9 %chunks.17 = bf16[2,512,512]{2,1,0:T(8,128)(2,1)S(1)} custom-call(s32[2]{0:T(128)S(1)} %pad_add_fusion.3.index_ref, bf16[512,512]{1,0:T(8,128)(2,1)S(1)} %attend.2.heads_ref, bf16[512,8192]{1,0:T(8,128)(2,1)} %bitcast.70, bf16[1,512,512]{2,1,0:T(8,128)(2,1)S(1)} %collective-permute-done.21.refs_0_, bf16[1,512,512]{2,1,0:T(8,128)(2,1)S(1)} %collective-permute-done.22.refs_1_), custom_call_target="tpu_custom_call" | custom-call | tf_op jit(solution)/shard_map/chunks/pallas_call | solution.py:458
  168.8 2.7 %collective-permute-start.26 = (bf16[2,512,512]{2,1,0:T(8,128)(2,1)S(1)}, bf16[2,512,512]{2,1,0:T(8,128)(2,1)S(1)}, u32[]{:S(2)}, u32[]{:S(2)}) collective-permute-start(bf16[2,512,512]{2,1,0:T(8,128)(2,1)S(1)} %chunks.17), channel_id=1, source_target_pairs={{0,2},{1,7},{2,4},{3,1},{4,6},{5,3},{6,0},{7,5},{8,10},{9,15},{10,... | collective-permute-start | bytes 3145736 | tf_op jit(solution)/shard_map/ppermute | solution.py:59
  171.4 3.0 %all-to-all-done.3 = bf16[16,16,512]{2,1,0:T(8,128)(2,1)S(1)} async-done(((bf16[16,16,512]{2,1,0:T(8,128)(2,1)}), bf16[16,16,512]{2,1,0:T(8,128)(2,1)S(1)}, u32[]{:S(2)}, u32[]{:S(2)}) %all-to-all-start.3) | async-done | bytes 262176 | tf_op jit(solution)/shard_map/all_to_all | solution.py:559
  175.5 3.1 %attend.3.heads_ref = bf16[512,512]{1,0:T(8,128)(2,1)S(1)} custom-call(s32[3,8]{1,0:T(4,128)S(1)} %pad_add_fusion.plan_ref, bf16[512,512]{1,0:T(8,128)(2,1)S(1)} %copy-done.11, bf16[256,512]{1,0:T(8,128)(2,1)S(1)} %bitcast.65, bf16[256,512]{1,0:T(8,128)(2,1)S(1)} %bitcast.68), custom_call_target="tpu_custom_call" | custom-call | tf_op jit(solution)/shard_map/attend/pallas_call | solution.py:389
  178.6 2.9 %chunks.18 = (bf16[1,512,512]{2,1,0:T(8,128)(2,1)S(1)}, bf16[1,512,512]{2,1,0:T(8,128)(2,1)S(1)}) custom-call(s32[2]{0:T(128)S(1)} %pad_add_fusion.4.index_ref, bf16[512,512]{1,0:T(8,128)(2,1)S(1)} %attend.3.heads_ref, bf16[512,8192]{1,0:T(8,128)(2,1)} %bitcast.71), custom_call_target="tpu_custom_call" | custom-call | tf_op jit(solution)/shard_map/chunks/pallas_call | solution.py:458
  185.0 2.9 %chunks.19 = bf16[2,512,512]{2,1,0:T(8,128)(2,1)S(1)} custom-call(s32[2]{0:T(128)S(1)} %pad_add_fusion.3.index_ref, bf16[512,512]{1,0:T(8,128)(2,1)S(1)} %attend.3.heads_ref, bf16[512,8192]{1,0:T(8,128)(2,1)} %bitcast.72, bf16[1,512,512]{2,1,0:T(8,128)(2,1)S(1)} %collective-permute-done.23.refs_0_, bf16[1,512,512]{2,1,0:T(8,128)(2,1)S(1)} %collective-permute-done.24.refs_1_), custom_call_target="tpu_custom_call" | custom-call | tf_op jit(solution)/shard_map/chunks/pallas_call | solution.py:458
  188.9 4.1 %chunks.20 = (bf16[1,512,512]{2,1,0:T(8,128)(2,1)S(1)}, bf16[1,512,512]{2,1,0:T(8,128)(2,1)S(1)}, bf16[1,512,512]{2,1,0:T(8,128)(2,1)S(1)}, bf16[1,512,512]{2,1,0:T(8,128)(2,1)S(1)}) custom-call(s32[4]{0:T(128)S(1)} %pad_add_fusion.2.index_ref, bf16[512,512]{1,0:T(8,128)(2,1)S(1)} %attend.2.heads_ref, bf16[512,8192]{1,0:T(8,128)(2,1)} %bitcast.73), custom_call_target="tpu_custom_call" | custom-call | tf_op jit(solution)/shard_map/chunks/pallas_call | solution.py:458
  197.3 4.3 %chunks.21 = (bf16[2,512,512]{2,1,0:T(8,128)(2,1)S(1)}, bf16[2,512,512]{2,1,0:T(8,128)(2,1)S(1)}) custom-call(s32[4]{0:T(128)S(1)} %pad_add_fusion.1.index_ref, bf16[512,512]{1,0:T(8,128)(2,1)S(1)} %attend.2.heads_ref, bf16[512,8192]{1,0:T(8,128)(2,1)} %bitcast.74, bf16[1,512,512]{2,1,0:T(8,128)(2,1)S(1)} %collective-permute-done.25.refs_0_, ...), custom_call_target="tpu_custom_call" | custom-call | tf_op jit(solution)/shard_map/chunks/pallas_call | solution.py:458
  201.6 2.2 collective-permute-start.35
  203.7 4.1 %chunks.22 = (bf16[1,512,512]{2,1,0:T(8,128)(2,1)S(1)}, bf16[1,512,512]{2,1,0:T(8,128)(2,1)S(1)}, bf16[1,512,512]{2,1,0:T(8,128)(2,1)S(1)}, bf16[1,512,512]{2,1,0:T(8,128)(2,1)S(1)}) custom-call(s32[4]{0:T(128)S(1)} %pad_add_fusion.2.index_ref, bf16[512,512]{1,0:T(8,128)(2,1)S(1)} %attend.3.heads_ref, bf16[512,8192]{1,0:T(8,128)(2,1)} %bitcast.75), custom_call_target="tpu_custom_call" | custom-call | tf_op jit(solution)/shard_map/chunks/pallas_call | solution.py:458
  212.1 4.3 %chunks.23 = (bf16[2,512,512]{2,1,0:T(8,128)(2,1)S(1)}, bf16[2,512,512]{2,1,0:T(8,128)(2,1)S(1)}) custom-call(s32[4]{0:T(128)S(1)} %pad_add_fusion.1.index_ref, bf16[512,512]{1,0:T(8,128)(2,1)S(1)} %attend.3.heads_ref, bf16[512,8192]{1,0:T(8,128)(2,1)} %bitcast.76, bf16[1,512,512]{2,1,0:T(8,128)(2,1)S(1)} %collective-permute-done.30.refs_0_, ...), custom_call_target="tpu_custom_call" | custom-call | tf_op jit(solution)/shard_map/chunks/pallas_call | solution.py:458
  219.5 1.8 collective-permute-start.40
  223.5 6.9 %collective-permute-done.37.refs_0_ = bf16[2,512,512]{2,1,0:T(8,128)(2,1)S(1)} collective-permute-done((bf16[2,512,512]{2,1,0:T(8,128)(2,1)S(1)}, bf16[2,512,512]{2,1,0:T(8,128)(2,1)S(1)}, u32[]{:S(2)}, u32[]{:S(2)}) %collective-permute-start.37) | collective-permute-done | bytes 1048608 | tf_op jit(solution)/shard_map/ppermute | solution.py:59
  232.1 2.3 collective-permute-start.39
  234.3 3.6 %collective-permute-done.38.refs_2_ = bf16[1,512,512]{2,1,0:T(8,128)(2,1)S(1)} collective-permute-done((bf16[1,512,512]{2,1,0:T(8,128)(2,1)S(1)}, bf16[1,512,512]{2,1,0:T(8,128)(2,1)S(1)}, u32[]{:S(2)}, u32[]{:S(2)}) %collective-permute-start.38) | collective-permute-done | bytes 524320 | tf_op jit(solution)/shard_map/ppermute | solution.py:59
  238.0 1.7 chunks.27
  239.7 1.9 collective-permute-done.40.refs_0_
  243.3 2.3 collective-permute-start.41
  247.1 2.5 chunks.29.refs_3_
  249.6 3.2 %collective-permute-done.42.refs_0_ = bf16[2,512,512]{2,1,0:T(8,128)(2,1)S(1)} collective-permute-done((bf16[2,512,512]{2,1,0:T(8,128)(2,1)S(1)}, bf16[2,512,512]{2,1,0:T(8,128)(2,1)S(1)}, u32[]{:S(2)}, u32[]{:S(2)}) %collective-permute-start.42) | collective-permute-done | bytes 1048608 | tf_op jit(solution)/shard_map/ppermute | solution.py:59
  254.5 2.3 collective-permute-start.43
  256.8 3.7 %collective-permute-done.44.refs_2_ = bf16[1,512,512]{2,1,0:T(8,128)(2,1)S(1)} collective-permute-done((bf16[1,512,512]{2,1,0:T(8,128)(2,1)S(1)}, bf16[1,512,512]{2,1,0:T(8,128)(2,1)S(1)}, u32[]{:S(2)}, u32[]{:S(2)}) %collective-permute-start.44) | collective-permute-done | bytes 524320 | tf_op jit(solution)/shard_map/ppermute | solution.py:59
  260.6 2.5 chunks.31
  (146 shorter events, 59.0 us)
Async XLA Ops:
  3.0 11.7 %all-to-all-start = ((s32[8,1,2]{2,1,0:T(1,128)}), s32[8,1,2]{2,1,0:T(1,128)S(1)}, u32[]{:S(2)}, u32[]{:S(2)}) async-start(s32[8,1,2]{2,1,0:T(1,128)} %copy.10), calls=%async_computation | async-start | bytes 8192 | tf_op jit(solution)/shard_map/all_to_all | solution.py:521
  14.7 30.5 %all-to-all-start.1 = ((bf16[8,272,512]{2,1,0:T(8,128)(2,1)}), bf16[8,272,512]{2,1,0:T(8,128)(2,1)S(1)}, u32[]{:S(2)}, u32[]{:S(2)}) async-start(bf16[8,272,512]{2,1,0:T(8,128)(2,1)} %cut.1), calls=%async_computation.1 | async-start | bytes 4456448 | tf_op jit(solution)/shard_map/all_to_all | solution.py:520
  49.3 8.1 %collective-permute-start.3 = (bf16[1024,512]{1,0:T(8,128)(2,1)S(1)}, bf16[1024,512]{1,0:T(8,128)(2,1)}, u32[]{:S(2)}, u32[]{:S(2)}) collective-permute-start(bf16[1024,512]{1,0:T(8,128)(2,1)S(1)} %pack.1), channel_id=1, source_target_pairs={{0,1},{1,0},{2,3},{3,2},{4,5},{5,4},{6,7},{7,6},{8,9},{9,8},{10,11... | collective-permute-start | bytes 3145736 | tf_op jit(solution)/shard_map/ppermute | solution.py:59
  52.1 14.5 %collective-permute-start = (bf16[1024,512]{1,0:T(8,128)(2,1)S(1)}, bf16[1024,512]{1,0:T(8,128)(2,1)S(1)}, u32[]{:S(2)}, u32[]{:S(2)}) collective-permute-start(bf16[1024,512]{1,0:T(8,128)(2,1)S(1)} %pack.1), channel_id=1, source_target_pairs={{0,2},{1,7},{2,4},{3,1},{4,6},{5,3},{6,0},{7,5},{8,10},{9,15},{10,... | collective-permute-start | bytes 3145736 | tf_op jit(solution)/shard_map/ppermute | solution.py:59
  54.9 25.8 %collective-permute-start.2 = (bf16[1024,512]{1,0:T(8,128)(2,1)S(1)}, bf16[1024,512]{1,0:T(8,128)(2,1)S(1)}, u32[]{:S(2)}, u32[]{:S(2)}) collective-permute-start(bf16[1024,512]{1,0:T(8,128)(2,1)S(1)} %pack.1), channel_id=1, source_target_pairs={{0,8},{1,9},{2,10},{3,11},{4,12},{5,13},{6,14},{7,15},{8,0},{9,1},... | collective-permute-start | bytes 3145736 | tf_op jit(solution)/shard_map/ppermute | solution.py:59
  57.4 23.3 %collective-permute-start.4 = (bf16[1024,512]{1,0:T(8,128)(2,1)}, bf16[1024,512]{1,0:T(8,128)(2,1)S(1)}, u32[]{:S(2)}, u32[]{:S(2)}) collective-permute-start(bf16[1024,512]{1,0:T(8,128)(2,1)} %collective-permute-done.3), channel_id=1, source_target_pairs={{0,2},{1,7},{2,4},{3,1},{4,6},{5,3},{6,0},{7,5},{8,10},{9,15},{10,... | collective-permute-start | bytes 3145736 | tf_op jit(solution)/shard_map/ppermute | solution.py:59
  80.7 7.2 %collective-permute-start.7 = (bf16[1024,512]{1,0:T(8,128)(2,1)S(1)}, bf16[1024,512]{1,0:T(8,128)(2,1)S(1)}, u32[]{:S(2)}, u32[]{:S(2)}) collective-permute-start(bf16[1024,512]{1,0:T(8,128)(2,1)S(1)} %collective-permute-done.2), channel_id=1, source_target_pairs={{0,1},{1,0},{2,3},{3,2},{4,5},{5,4},{6,7},{7,6},{8,9},{9,8},{10,11... | collective-permute-start | bytes 3145736 | tf_op jit(solution)/shard_map/ppermute | solution.py:59
  80.9 8.5 %collective-permute-start.5 = (bf16[1024,512]{1,0:T(8,128)(2,1)S(1)}, bf16[1024,512]{1,0:T(8,128)(2,1)S(1)}, u32[]{:S(2)}, u32[]{:S(2)}) collective-permute-start(bf16[1024,512]{1,0:T(8,128)(2,1)S(1)} %collective-permute-done), channel_id=1, source_target_pairs={{0,1},{1,0},{2,3},{3,2},{4,5},{5,4},{6,7},{7,6},{8,9},{9,8},{10,11... | collective-permute-start | bytes 3145736 | tf_op jit(solution)/shard_map/ppermute | solution.py:59
  81.2 9.3 %collective-permute-start.6 = (bf16[1024,512]{1,0:T(8,128)(2,1)S(1)}, bf16[1024,512]{1,0:T(8,128)(2,1)S(1)}, u32[]{:S(2)}, u32[]{:S(2)}) collective-permute-start(bf16[1024,512]{1,0:T(8,128)(2,1)S(1)} %collective-permute-done.4), channel_id=1, source_target_pairs={{0,1},{1,0},{2,3},{3,2},{4,5},{5,4},{6,7},{7,6},{8,9},{9,8},{10,11... | collective-permute-start | bytes 3145736 | tf_op jit(solution)/shard_map/ppermute | solution.py:59
  81.4 26.1 %collective-permute-start.1 = (bf16[1024,512]{1,0:T(8,128)(2,1)S(1)}, bf16[1024,512]{1,0:T(8,128)(2,1)}, u32[]{:S(2)}, u32[]{:S(2)}) collective-permute-start(bf16[1024,512]{1,0:T(8,128)(2,1)S(1)} %collective-permute-done), channel_id=1, source_target_pairs={{0,2},{1,7},{2,4},{3,1},{4,6},{5,3},{6,0},{7,5},{8,10},{9,15},{10,... | collective-permute-start | bytes 3145736 | tf_op jit(solution)/shard_map/ppermute | solution.py:59
  83.8 25.6 %collective-permute-start.10 = (bf16[512,512]{1,0:T(8,128)(2,1)}, bf16[512,512]{1,0:T(8,128)(2,1)}, u32[]{:S(2)}, u32[]{:S(2)}) collective-permute-start(bf16[512,512]{1,0:T(8,128)(2,1)} %slice.39), channel_id=1, source_target_pairs={{0,8},{1,9},{2,10},{3,11},{4,12},{5,13},{6,14},{7,15},{8,0},{9,1},... | collective-permute-start | bytes 1572872 | tf_op jit(solution)/shard_map/ppermute | solution.py:59
  87.9 21.8 %collective-permute-start.11 = (bf16[512,512]{1,0:T(8,128)(2,1)}, bf16[512,512]{1,0:T(8,128)(2,1)}, u32[]{:S(2)}, u32[]{:S(2)}) collective-permute-start(bf16[512,512]{1,0:T(8,128)(2,1)} %slice.37), channel_id=1, source_target_pairs={{0,8},{1,9},{2,10},{3,11},{4,12},{5,13},{6,14},{7,15},{8,0},{9,1},... | collective-permute-start | bytes 1572872 | tf_op jit(solution)/shard_map/ppermute | solution.py:59
  90.3 19.4 %collective-permute-start.8 = (bf16[512,512]{1,0:T(8,128)(2,1)}, bf16[512,512]{1,0:T(8,128)(2,1)}, u32[]{:S(2)}, u32[]{:S(2)}) collective-permute-start(bf16[512,512]{1,0:T(8,128)(2,1)} %slice.34), channel_id=1, source_target_pairs={{0,2},{1,7},{2,4},{3,1},{4,6},{5,3},{6,0},{7,5},{8,10},{9,15},{10,... | collective-permute-start | bytes 1572872 | tf_op jit(solution)/shard_map/ppermute | solution.py:59
  91.5 18.3 %collective-permute-start.9 = (bf16[512,512]{1,0:T(8,128)(2,1)}, bf16[512,512]{1,0:T(8,128)(2,1)}, u32[]{:S(2)}, u32[]{:S(2)}) collective-permute-start(bf16[512,512]{1,0:T(8,128)(2,1)} %slice.38), channel_id=1, source_target_pairs={{0,2},{1,7},{2,4},{3,1},{4,6},{5,3},{6,0},{7,5},{8,10},{9,15},{10,... | collective-permute-start | bytes 1572872 | tf_op jit(solution)/shard_map/ppermute | solution.py:59
  109.7 6.2 %collective-permute-start.14 = (bf16[1024,512]{1,0:T(8,128)(2,1)}, bf16[1024,512]{1,0:T(8,128)(2,1)S(1)}, u32[]{:S(2)}, u32[]{:S(2)}) collective-permute-start(bf16[1024,512]{1,0:T(8,128)(2,1)} %collective-permute-done.1.refs_0_), channel_id=1, source_target_pairs={{0,1},{1,0},{2,3},{3,2},{4,5},{5,4},{6,7},{7,6},{8,9},{9,8},{10,11... | collective-permute-start | bytes 3145736 | tf_op jit(solution)/shard_map/ppermute | solution.py:59
  111.5 4.4 %collective-permute-start.15 = (bf16[512,512]{1,0:T(8,128)(2,1)}, bf16[512,512]{1,0:T(8,128)(2,1)}, u32[]{:S(2)}, u32[]{:S(2)}) collective-permute-start(bf16[512,512]{1,0:T(8,128)(2,1)} %collective-permute-done.8.refs_2_), channel_id=1, source_target_pairs={{0,1},{1,0},{2,3},{3,2},{4,5},{5,4},{6,7},{7,6},{8,9},{9,8},{10,11... | collective-permute-start | bytes 1572872 | tf_op jit(solution)/shard_map/ppermute | solution.py:59
  111.6 4.4 %collective-permute-start.16 = (bf16[512,512]{1,0:T(8,128)(2,1)}, bf16[512,512]{1,0:T(8,128)(2,1)}, u32[]{:S(2)}, u32[]{:S(2)}) collective-permute-start(bf16[512,512]{1,0:T(8,128)(2,1)} %collective-permute-done.9.refs_3_), channel_id=1, source_target_pairs={{0,1},{1,0},{2,3},{3,2},{4,5},{5,4},{6,7},{7,6},{8,9},{9,8},{10,11... | collective-permute-start | bytes 1572872 | tf_op jit(solution)/shard_map/ppermute | solution.py:59
  112.0 12.0 %collective-permute-start.13 = (bf16[512,512]{1,0:T(8,128)(2,1)}, bf16[512,512]{1,0:T(8,128)(2,1)S(1)}, u32[]{:S(2)}, u32[]{:S(2)}) collective-permute-start(bf16[512,512]{1,0:T(8,128)(2,1)} %collective-permute-done.8.refs_2_), channel_id=1, source_target_pairs={{0,2},{1,7},{2,4},{3,1},{4,6},{5,3},{6,0},{7,5},{8,10},{9,15},{10,... | collective-permute-start | bytes 1572872 | tf_op jit(solution)/shard_map/ppermute | solution.py:59
  113.5 14.9 %collective-permute-start.12 = (bf16[512,512]{1,0:T(8,128)(2,1)}, bf16[512,512]{1,0:T(8,128)(2,1)S(1)}, u32[]{:S(2)}, u32[]{:S(2)}) collective-permute-start(bf16[512,512]{1,0:T(8,128)(2,1)} %slice.33), channel_id=1, source_target_pairs={{0,8},{1,9},{2,10},{3,11},{4,12},{5,13},{6,14},{7,15},{8,0},{9,1},... | collective-permute-start | bytes 1572872 | tf_op jit(solution)/shard_map/ppermute | solution.py:59
  124.0 4.4 %collective-permute-start.17 = (bf16[512,512]{1,0:T(8,128)(2,1)S(1)}, bf16[512,512]{1,0:T(8,128)(2,1)}, u32[]{:S(2)}, u32[]{:S(2)}) collective-permute-start(bf16[512,512]{1,0:T(8,128)(2,1)S(1)} %collective-permute-done.13.refs_0_), channel_id=1, source_target_pairs={{0,1},{1,0},{2,3},{3,2},{4,5},{5,4},{6,7},{7,6},{8,9},{9,8},{10,11... | collective-permute-start | bytes 1572872 | tf_op jit(solution)/shard_map/ppermute | solution.py:59
  124.7 16.5 %collective-permute-start.18 = (bf16[512,512]{1,0:T(8,128)(2,1)}, bf16[512,512]{1,0:T(8,128)(2,1)S(1)}, u32[]{:S(2)}, u32[]{:S(2)}) collective-permute-start(bf16[512,512]{1,0:T(8,128)(2,1)} %collective-permute-done.10.refs_2_), channel_id=1, source_target_pairs={{0,1},{1,0},{2,3},{3,2},{4,5},{5,4},{6,7},{7,6},{8,9},{9,8},{10,11... | collective-permute-start | bytes 1572872 | tf_op jit(solution)/shard_map/ppermute | solution.py:59
  124.7 16.5 %collective-permute-start.19 = (bf16[512,512]{1,0:T(8,128)(2,1)}, bf16[512,512]{1,0:T(8,128)(2,1)S(1)}, u32[]{:S(2)}, u32[]{:S(2)}) collective-permute-start(bf16[512,512]{1,0:T(8,128)(2,1)} %collective-permute-done.11.refs_3_), channel_id=1, source_target_pairs={{0,1},{1,0},{2,3},{3,2},{4,5},{5,4},{6,7},{7,6},{8,9},{9,8},{10,11... | collective-permute-start | bytes 1572872 | tf_op jit(solution)/shard_map/ppermute | solution.py:59
  134.2 7.1 %collective-permute-start.20 = (bf16[512,512]{1,0:T(8,128)(2,1)S(1)}, bf16[512,512]{1,0:T(8,128)(2,1)S(1)}, u32[]{:S(2)}, u32[]{:S(2)}) collective-permute-start(bf16[512,512]{1,0:T(8,128)(2,1)S(1)} %copy-done.15), channel_id=1, source_target_pairs={{0,1},{1,0},{2,3},{3,2},{4,5},{5,4},{6,7},{7,6},{8,9},{9,8},{10,11... | collective-permute-start | bytes 1572872 | tf_op jit(solution)/shard_map/ppermute | solution.py:59
  135.4 17.1 %all-to-all-start.2 = ((bf16[16,16,512]{2,1,0:T(8,128)(2,1)}), bf16[16,16,512]{2,1,0:T(8,128)(2,1)S(1)}, u32[]{:S(2)}, u32[]{:S(2)}) async-start(bf16[16,16,512]{2,1,0:T(8,128)(2,1)} %get-tuple-element.82), calls=%async_computation.2 | async-start | bytes 524288 | tf_op jit(solution)/shard_map/all_to_all | solution.py:559
  158.0 7.9 %collective-permute-start.21 = (bf16[1,512,512]{2,1,0:T(8,128)(2,1)S(1)}, bf16[1,512,512]{2,1,0:T(8,128)(2,1)S(1)}, u32[]{:S(2)}, u32[]{:S(2)}) collective-permute-start(bf16[1,512,512]{2,1,0:T(8,128)(2,1)S(1)} %get-tuple-element.84), channel_id=1, source_target_pairs={{0,1},{1,0},{2,3},{3,2},{4,5},{5,4},{6,7},{7,6},{8,9},{9,8},{10,11... | collective-permute-start | bytes 1572872 | tf_op jit(solution)/shard_map/ppermute | solution.py:59
  158.1 7.7 %collective-permute-start.22 = (bf16[1,512,512]{2,1,0:T(8,128)(2,1)S(1)}, bf16[1,512,512]{2,1,0:T(8,128)(2,1)S(1)}, u32[]{:S(2)}, u32[]{:S(2)}) collective-permute-start(bf16[1,512,512]{2,1,0:T(8,128)(2,1)S(1)} %get-tuple-element.86), channel_id=1, source_target_pairs={{0,1},{1,0},{2,3},{3,2},{4,5},{5,4},{6,7},{7,6},{8,9},{9,8},{10,11... | collective-permute-start | bytes 1572872 | tf_op jit(solution)/shard_map/ppermute | solution.py:59
  158.5 15.9 %all-to-all-start.3 = ((bf16[16,16,512]{2,1,0:T(8,128)(2,1)}), bf16[16,16,512]{2,1,0:T(8,128)(2,1)S(1)}, u32[]{:S(2)}, u32[]{:S(2)}) async-start(bf16[16,16,512]{2,1,0:T(8,128)(2,1)} %get-tuple-element.89), calls=%async_computation.3 | async-start | bytes 524288 | tf_op jit(solution)/shard_map/all_to_all | solution.py:559
  168.8 24.9 %collective-permute-start.26 = (bf16[2,512,512]{2,1,0:T(8,128)(2,1)S(1)}, bf16[2,512,512]{2,1,0:T(8,128)(2,1)S(1)}, u32[]{:S(2)}, u32[]{:S(2)}) collective-permute-start(bf16[2,512,512]{2,1,0:T(8,128)(2,1)S(1)} %chunks.17), channel_id=1, source_target_pairs={{0,2},{1,7},{2,4},{3,1},{4,6},{5,3},{6,0},{7,5},{8,10},{9,15},{10,... | collective-permute-start | bytes 3145736 | tf_op jit(solution)/shard_map/ppermute | solution.py:59
  181.4 2.8 %collective-permute-start.23 = (bf16[1,512,512]{2,1,0:T(8,128)(2,1)S(1)}, bf16[1,512,512]{2,1,0:T(8,128)(2,1)S(1)}, u32[]{:S(2)}, u32[]{:S(2)}) collective-permute-start(bf16[1,512,512]{2,1,0:T(8,128)(2,1)S(1)} %get-tuple-element.91), channel_id=1, source_target_pairs={{0,1},{1,0},{2,3},{3,2},{4,5},{5,4},{6,7},{7,6},{8,9},{9,8},{10,11... | collective-permute-start | bytes 1572872 | tf_op jit(solution)/shard_map/ppermute | solution.py:59
  182.7 2.3 collective-permute-start.24
  187.9 20.6 %collective-permute-start.31 = (bf16[2,512,512]{2,1,0:T(8,128)(2,1)S(1)}, bf16[2,512,512]{2,1,0:T(8,128)(2,1)S(1)}, u32[]{:S(2)}, u32[]{:S(2)}) collective-permute-start(bf16[2,512,512]{2,1,0:T(8,128)(2,1)S(1)} %chunks.19), channel_id=1, source_target_pairs={{0,2},{1,7},{2,4},{3,1},{4,6},{5,3},{6,0},{7,5},{8,10},{9,15},{10,... | collective-permute-start | bytes 3145736 | tf_op jit(solution)/shard_map/ppermute | solution.py:59
  193.0 2.0 collective-permute-start.25
  193.1 2.6 %collective-permute-start.27 = (bf16[1,512,512]{2,1,0:T(8,128)(2,1)S(1)}, bf16[1,512,512]{2,1,0:T(8,128)(2,1)S(1)}, u32[]{:S(2)}, u32[]{:S(2)}) collective-permute-start(bf16[1,512,512]{2,1,0:T(8,128)(2,1)S(1)} %get-tuple-element.97), channel_id=1, source_target_pairs={{0,1},{1,0},{2,3},{3,2},{4,5},{5,4},{6,7},{7,6},{8,9},{9,8},{10,11... | collective-permute-start | bytes 1572872 | tf_op jit(solution)/shard_map/ppermute | solution.py:59
  193.6 2.9 %collective-permute-start.28 = (bf16[1,512,512]{2,1,0:T(8,128)(2,1)S(1)}, bf16[1,512,512]{2,1,0:T(8,128)(2,1)S(1)}, u32[]{:S(2)}, u32[]{:S(2)}) collective-permute-start(bf16[1,512,512]{2,1,0:T(8,128)(2,1)S(1)} %get-tuple-element.98), channel_id=1, source_target_pairs={{0,1},{1,0},{2,3},{3,2},{4,5},{5,4},{6,7},{7,6},{8,9},{9,8},{10,11... | collective-permute-start | bytes 1572872 | tf_op jit(solution)/shard_map/ppermute | solution.py:59
  193.7 3.6 %collective-permute-start.29 = (bf16[1,512,512]{2,1,0:T(8,128)(2,1)S(1)}, bf16[1,512,512]{2,1,0:T(8,128)(2,1)S(1)}, u32[]{:S(2)}, u32[]{:S(2)}) collective-permute-start(bf16[1,512,512]{2,1,0:T(8,128)(2,1)S(1)} %get-tuple-element.99), channel_id=1, source_target_pairs={{0,1},{1,0},{2,3},{3,2},{4,5},{5,4},{6,7},{7,6},{8,9},{9,8},{10,11... | collective-permute-start | bytes 1572872 | tf_op jit(solution)/shard_map/ppermute | solution.py:59
  201.6 15.5 %collective-permute-start.35 = (bf16[2,512,512]{2,1,0:T(8,128)(2,1)S(1)}, bf16[2,512,512]{2,1,0:T(8,128)(2,1)S(1)}, u32[]{:S(2)}, u32[]{:S(2)}) collective-permute-start(bf16[2,512,512]{2,1,0:T(8,128)(2,1)S(1)} %get-tuple-element.100), channel_id=1, source_target_pairs={{0,2},{1,7},{2,4},{3,1},{4,6},{5,3},{6,0},{7,5},{8,10},{9,15},{10,... | collective-permute-start | bytes 3145736 | tf_op jit(solution)/shard_map/ppermute | solution.py:59
  207.9 2.6 %collective-permute-start.32 = (bf16[1,512,512]{2,1,0:T(8,128)(2,1)S(1)}, bf16[1,512,512]{2,1,0:T(8,128)(2,1)S(1)}, u32[]{:S(2)}, u32[]{:S(2)}) collective-permute-start(bf16[1,512,512]{2,1,0:T(8,128)(2,1)S(1)} %get-tuple-element.104), channel_id=1, source_target_pairs={{0,1},{1,0},{2,3},{3,2},{4,5},{5,4},{6,7},{7,6},{8,9},{9,8},{10,11... | collective-permute-start | bytes 1572872 | tf_op jit(solution)/shard_map/ppermute | solution.py:59
  208.4 2.9 %collective-permute-start.33 = (bf16[1,512,512]{2,1,0:T(8,128)(2,1)S(1)}, bf16[1,512,512]{2,1,0:T(8,128)(2,1)S(1)}, u32[]{:S(2)}, u32[]{:S(2)}) collective-permute-start(bf16[1,512,512]{2,1,0:T(8,128)(2,1)S(1)} %get-tuple-element.105), channel_id=1, source_target_pairs={{0,1},{1,0},{2,3},{3,2},{4,5},{5,4},{6,7},{7,6},{8,9},{9,8},{10,11... | collective-permute-start | bytes 1572872 | tf_op jit(solution)/shard_map/ppermute | solution.py:59
  208.5 3.6 %collective-permute-start.34 = (bf16[1,512,512]{2,1,0:T(8,128)(2,1)S(1)}, bf16[1,512,512]{2,1,0:T(8,128)(2,1)S(1)}, u32[]{:S(2)}, u32[]{:S(2)}) collective-permute-start(bf16[1,512,512]{2,1,0:T(8,128)(2,1)S(1)} %get-tuple-element.106), channel_id=1, source_target_pairs={{0,1},{1,0},{2,3},{3,2},{4,5},{5,4},{6,7},{7,6},{8,9},{9,8},{10,11... | collective-permute-start | bytes 1572872 | tf_op jit(solution)/shard_map/ppermute | solution.py:59
  216.4 14.0 %collective-permute-start.37 = (bf16[2,512,512]{2,1,0:T(8,128)(2,1)S(1)}, bf16[2,512,512]{2,1,0:T(8,128)(2,1)S(1)}, u32[]{:S(2)}, u32[]{:S(2)}) collective-permute-start(bf16[2,512,512]{2,1,0:T(8,128)(2,1)S(1)} %get-tuple-element.107), channel_id=1, source_target_pairs={{0,2},{1,7},{2,4},{3,1},{4,6},{5,3},{6,0},{7,5},{8,10},{9,15},{10,... | collective-permute-start | bytes 3145736 | tf_op jit(solution)/shard_map/ppermute | solution.py:59
  218.7 2.5 collective-permute-start.36
  219.5 22.1 %collective-permute-start.40 = (bf16[2,512,512]{2,1,0:T(8,128)(2,1)S(1)}, bf16[2,512,512]{2,1,0:T(8,128)(2,1)S(1)}, u32[]{:S(2)}, u32[]{:S(2)}) collective-permute-start(bf16[2,512,512]{2,1,0:T(8,128)(2,1)S(1)} %get-tuple-element.114), channel_id=1, source_target_pairs={{0,2},{1,7},{2,4},{3,1},{4,6},{5,3},{6,0},{7,5},{8,10},{9,15},{10,... | collective-permute-start | bytes 3145736 | tf_op jit(solution)/shard_map/ppermute | solution.py:59
  223.0 15.0 %collective-permute-start.38 = (bf16[1,512,512]{2,1,0:T(8,128)(2,1)S(1)}, bf16[1,512,512]{2,1,0:T(8,128)(2,1)S(1)}, u32[]{:S(2)}, u32[]{:S(2)}) collective-permute-start(bf16[1,512,512]{2,1,0:T(8,128)(2,1)S(1)} %chunks.25), channel_id=1, source_target_pairs={{0,8},{1,9},{2,10},{3,11},{4,12},{5,13},{6,14},{7,15},{8,0},{9,1},... | collective-permute-start | bytes 1572872 | tf_op jit(solution)/shard_map/ppermute | solution.py:59
  232.1 5.9 %collective-permute-start.39 = (bf16[1,512,512]{2,1,0:T(8,128)(2,1)S(1)}, bf16[1,512,512]{2,1,0:T(8,128)(2,1)S(1)}, u32[]{:S(2)}, u32[]{:S(2)}) collective-permute-start(bf16[1,512,512]{2,1,0:T(8,128)(2,1)S(1)} %chunks.26), channel_id=1, source_target_pairs={{0,1},{1,0},{2,3},{3,2},{4,5},{5,4},{6,7},{7,6},{8,9},{9,8},{10,11... | collective-permute-start | bytes 1572872 | tf_op jit(solution)/shard_map/ppermute | solution.py:59
  234.3 18.5 %collective-permute-start.42 = (bf16[2,512,512]{2,1,0:T(8,128)(2,1)S(1)}, bf16[2,512,512]{2,1,0:T(8,128)(2,1)S(1)}, u32[]{:S(2)}, u32[]{:S(2)}) collective-permute-start(bf16[2,512,512]{2,1,0:T(8,128)(2,1)S(1)} %get-tuple-element.117), channel_id=1, source_target_pairs={{0,2},{1,7},{2,4},{3,1},{4,6},{5,3},{6,0},{7,5},{8,10},{9,15},{10,... | collective-permute-start | bytes 3145736 | tf_op jit(solution)/shard_map/ppermute | solution.py:59
  243.3 3.8 %collective-permute-start.41 = (bf16[1,512,512]{2,1,0:T(8,128)(2,1)S(1)}, bf16[1,512,512]{2,1,0:T(8,128)(2,1)S(1)}, u32[]{:S(2)}, u32[]{:S(2)}) collective-permute-start(bf16[1,512,512]{2,1,0:T(8,128)(2,1)S(1)} %chunks.28), channel_id=1, source_target_pairs={{0,1},{1,0},{2,3},{3,2},{4,5},{5,4},{6,7},{7,6},{8,9},{9,8},{10,11... | collective-permute-start | bytes 1572872 | tf_op jit(solution)/shard_map/ppermute | solution.py:59
  245.6 15.0 %collective-permute-start.44 = (bf16[1,512,512]{2,1,0:T(8,128)(2,1)S(1)}, bf16[1,512,512]{2,1,0:T(8,128)(2,1)S(1)}, u32[]{:S(2)}, u32[]{:S(2)}) collective-permute-start(bf16[1,512,512]{2,1,0:T(8,128)(2,1)S(1)} %chunks.27), channel_id=1, source_target_pairs={{0,8},{1,9},{2,10},{3,11},{4,12},{5,13},{6,14},{7,15},{8,0},{9,1},... | collective-permute-start | bytes 1572872 | tf_op jit(solution)/shard_map/ppermute | solution.py:59
  254.5 6.0 %collective-permute-start.43 = (bf16[1,512,512]{2,1,0:T(8,128)(2,1)S(1)}, bf16[1,512,512]{2,1,0:T(8,128)(2,1)S(1)}, u32[]{:S(2)}, u32[]{:S(2)}) collective-permute-start(bf16[1,512,512]{2,1,0:T(8,128)(2,1)S(1)} %chunks.30), channel_id=1, source_target_pairs={{0,1},{1,0},{2,3},{3,2},{4,5},{5,4},{6,7},{7,6},{8,9},{9,8},{10,11... | collective-permute-start | bytes 1572872 | tf_op jit(solution)/shard_map/ppermute | solution.py:59
  (20 other events, 38.2 us)
where the time goes:
time: 265 us; the launch traced here: 263 us
  Pallas kernels  92.3 us (35%)
  waiting for transfers between devices  72 us (27%)
  starting transfers between devices  66.9 us (25%)
  local copies, waits for them, and re-layouts  22.9 us (9%)
  other arithmetic  8.58 us (3%)
    ppermute x45, starting transfers between devices, send(): return lax.ppermute(value, 'tp', pairs)  43.4 us
    pallas_call x16, Pallas kernels, chunks(): pl.pallas_call(functools.partial(chunks_kernel, groups, tuple((len(a) for...  43.3 us
    ppermute x45, waiting for transfers between devices, send(): return lax.ppermute(value, 'tp', pairs)  41.4 us
    all_to_all x1, waiting for transfers between devices, body(): lax.all_to_all(outgoing, 'sec', split_axis=0, concat_axis=0, tiled=True)  26.3 us
    pallas_call x3, Pallas kernels, project_block(): pl.pallas_call(functools.partial(project_block_kernel, tuple(skips), last...  19.7 us
    pallas_call x2, Pallas kernels, project(): pl.pallas_call(functools.partial(project_kernel, counts, total is not Non...  17.5 us
    unnamed x38, local copies, waits for them, and re-layouts  16.6 us
    all_to_all x2, starting transfers between devices, spread(): lax.all_to_all(line.next(keyval), 'tp', split_axis=0, concat_axis=0, tile...  12.8 us
  transfers between devices with their start and end apart: 49, of which 23 were waited for; matrix products, arithmetic and copies ran while one was open for 5% of the time, Pallas kernels for 31%

commit v1 on v0

--- a/solution.py
+++ b/solution.py
@@ -631,9 +631,8 @@
     total0 = projected_block(pieces, order[8:14], 0, total)[0]
     there_far0, far = join(there_far0, far)
     pieces = [there_far0, send(there_far0, TO_CORE)]
-    index = after(order[14:], there_far1)
-    query0, keyval0 = projected_block(pieces, index, 0, total0, tables)
-    keyval0 = spread(keyval0)
+    query0, keyval0 = projected_block(pieces, order[14:], 0, total0, tables)
+    keyval0 = spread(after(keyval0, there_far1))
     pieces = [far, far_other, *there_up[2:], *there_down[2:]]
     pieces += [there_far1, move(there_far1, TO_CORE)]
     query1, keyval1 = projected_block(pieces, order[8:], 1, total, tables)

time: 265 us -> 270 us (1.019)
  waiting for transfers between devices: 72 us -> 76.9 us
    ppermute x45, waiting for transfers between devices: 41.4 us -> 46.3 us  [send(): return lax.ppermute(value, 'tp', pairs)]
    unnamed x38 -> x40, local copies, waits for them, and re-layouts: 16.6 us -> 17.3 us
  transfers between devices with their start and end apart: 49 -> 49, of which waited for: 23 -> 25; matrix products, arithmetic and copies ran while one was open for 5% -> 4% of each run, Pallas kernels for 31% -> 30%
where the time goes in v1:
time: 270 us; the launch traced here: 268 us
  Pallas kernels  92.3 us (34%)
  waiting for transfers between devices  76.9 us (28%)
  starting transfers between devices  66.2 us (25%)
  local copies, waits for them, and re-layouts  23.6 us (9%)
  other arithmetic  8.61 us (3%)
    ppermute x45, waiting for transfers between devices, send(): return lax.ppermute(value, 'tp', pairs)  46.3 us
    pallas_call x16, Pallas kernels, chunks(): pl.pallas_call(functools.partial(chunks_kernel, groups, tuple((len(a) for...  43.3 us
    ppermute x45, starting transfers between devices, send(): return lax.ppermute(value, 'tp', pairs)  43.1 us
    all_to_all x1, waiting for transfers between devices, body(): lax.all_to_all(outgoing, 'sec', split_axis=0, concat_axis=0, tiled=True)  26.3 us
    pallas_call x3, Pallas kernels, project_block(): pl.pallas_call(functools.partial(project_block_kernel, tuple(skips), last...  19.7 us
    pallas_call x2, Pallas kernels, project(): pl.pallas_call(functools.partial(project_kernel, counts, total is not Non...  17.5 us
    unnamed x40, local copies, waits for them, and re-layouts  17.3 us
    all_to_all x2, starting transfers between devices, spread(): lax.all_to_all(line.next(keyval), 'tp', split_axis=0, concat_axis=0, tile...  12.5 us
  transfers between devices with their start and end apart: 49, of which 25 were waited for; matrix products, arithmetic and copies ran while one was open for 4% of the time, Pallas kernels for 30%

profile of v1, /device:TPU:1, one launch (start us, length us, event | category | flops | bytes accessed | tf_op | source)
XLA Modules:
  0.0 268.3 jit_solution(16191911173665940463)
XLA Ops:
  3.0 6.8 %all-to-all-start = ((s32[8,1,2]{2,1,0:T(1,128)}), s32[8,1,2]{2,1,0:T(1,128)S(1)}, u32[]{:S(2)}, u32[]{:S(2)}) async-start(s32[8,1,2]{2,1,0:T(1,128)} %copy.10), calls=%async_computation | async-start | bytes 8192 | tf_op jit(solution)/shard_map/all_to_all | solution.py:521
  11.4 2.0 cut.1
  14.7 3.9 %all-to-all-start.1 = ((bf16[8,272,512]{2,1,0:T(8,128)(2,1)}), bf16[8,272,512]{2,1,0:T(8,128)(2,1)S(1)}, u32[]{:S(2)}, u32[]{:S(2)}) async-start(bf16[8,272,512]{2,1,0:T(8,128)(2,1)} %cut.1), calls=%async_computation.1 | async-start | bytes 4456448 | tf_op jit(solution)/shard_map/all_to_all | solution.py:520
  18.9 26.3 %all-to-all-done.1.arrived_ref = bf16[8,272,512]{2,1,0:T(8,128)(2,1)S(1)} async-done(((bf16[8,272,512]{2,1,0:T(8,128)(2,1)}), bf16[8,272,512]{2,1,0:T(8,128)(2,1)S(1)}, u32[]{:S(2)}, u32[]{:S(2)}) %all-to-all-start.1) | async-done | bytes 2228256 | tf_op jit(solution)/shard_map/all_to_all | solution.py:520
  45.2 4.0 %pack.1 = bf16[1024,512]{1,0:T(8,128)(2,1)S(1)} custom-call(s32[3,8]{1,0:T(4,128)S(1)} %pad_add_fusion.plan_ref, bf16[8,272,512]{2,1,0:T(8,128)(2,1)S(1)} %all-to-all-done.1.arrived_ref), custom_call_target="tpu_custom_call" | custom-call | tf_op jit(solution)/shard_map/pack/pallas_call | solution.py:111
  49.3 2.8 %collective-permute-start.3 = (bf16[1024,512]{1,0:T(8,128)(2,1)S(1)}, bf16[1024,512]{1,0:T(8,128)(2,1)}, u32[]{:S(2)}, u32[]{:S(2)}) collective-permute-start(bf16[1024,512]{1,0:T(8,128)(2,1)S(1)} %pack.1), channel_id=1, source_target_pairs={{0,1},{1,0},{2,3},{3,2},{4,5},{5,4},{6,7},{7,6},{8,9},{9,8},{10,11... | collective-permute-start | bytes 3145736 | tf_op jit(solution)/shard_map/ppermute | solution.py:59
  52.1 2.8 %collective-permute-start = (bf16[1024,512]{1,0:T(8,128)(2,1)S(1)}, bf16[1024,512]{1,0:T(8,128)(2,1)S(1)}, u32[]{:S(2)}, u32[]{:S(2)}) collective-permute-start(bf16[1024,512]{1,0:T(8,128)(2,1)S(1)} %pack.1), channel_id=1, source_target_pairs={{0,2},{1,7},{2,4},{3,1},{4,6},{5,3},{6,0},{7,5},{8,10},{9,15},{10,... | collective-permute-start | bytes 3145736 | tf_op jit(solution)/shard_map/ppermute | solution.py:59
  54.9 2.5 collective-permute-start.2
  58.0 5.5 %fusion.3 = (f32[1024,128]{1,0:T(8,128)}, f32[1024,128]{1,0:T(8,128)}, f32[1024,128]{1,0:T(8,128)}, f32[1024,128]{1,0:T(8,128)}) fusion(f32[128]{0:T(128)S(1)} %fusion.9, f32[128]{0:T(128)S(1)} %get-tuple-element.127, f32[1024]{0:T(1024)S(1)} %subtract_convert_fusion, pred[]{:T(512)S(6)} %lt.136, f32[128]{0:T(128)S(1)} %get-tuple-element.128), kind=kLoop, calls=%fused_computation.7 | loop fusion | flops 786432 | bytes 2102785 | tf_op jit(solution)/shard_map/jit(_where)/select_n | solution.py:505
  63.5 3.1 %collective-permute-done = bf16[1024,512]{1,0:T(8,128)(2,1)S(1)} collective-permute-done((bf16[1024,512]{1,0:T(8,128)(2,1)S(1)}, bf16[1024,512]{1,0:T(8,128)(2,1)S(1)}, u32[]{:S(2)}, u32[]{:S(2)}) %collective-permute-start) | collective-permute-done | bytes 1048608 | tf_op jit(solution)/shard_map/ppermute | solution.py:59
  66.6 6.9 %project.2.refs_7_ = f32[1024,640]{1,0:T(8,128)S(1)} custom-call(s32[3]{0:T(128)S(1)} %pad_add_fusion.6.index_ref, bf16[1,1024,512]{2,1,0:T(8,128)(2,1)S(1)} %bitcast.59, bf16[1,1024,512]{2,1,0:T(8,128)(2,1)} %bitcast.28.refs_1_, bf16[1,1024,512]{2,1,0:T(8,128)(2,1)S(1)} %bitcast.60, bf16[8192,512]{1,0:T(8,128)(2,1)} %bitcast.85, bf16[8192,128]{1,0:T(8,128)(2,1)} %bitcast.90), custom_call_target="tpu_custom_call" | custom-call | tf_op jit(solution)/shard_map/project/pallas_call | solution.py:236
  75.0 5.7 %collective-permute-done.2 = bf16[1024,512]{1,0:T(8,128)(2,1)S(1)} collective-permute-done((bf16[1024,512]{1,0:T(8,128)(2,1)S(1)}, bf16[1024,512]{1,0:T(8,128)(2,1)S(1)}, u32[]{:S(2)}, u32[]{:S(2)}) %collective-permute-start.2) | collective-permute-done | bytes 1048608 | tf_op jit(solution)/shard_map/ppermute | solution.py:59
  83.8 2.5 collective-permute-start.10
  95.5 10.6 %project.3.refs_8_.refs_10_ = f32[1024,640]{1,0:T(8,128)S(1)} custom-call(s32[5]{0:T(128)S(1)} %stack.145.index_ref, bf16[1,1024,512]{2,1,0:T(8,128)(2,1)S(1)} %bitcast.62, bf16[1,1024,512]{2,1,0:T(8,128)(2,1)S(1)} %bitcast.66, bf16[1,1024,512]{2,1,0:T(8,128)(2,1)S(1)} %bitcast.67, bf16[1,1024,512]{2,1,0:T(8,128)(2,1)S(1)} %bitcast.61, ...), custom_call_target="tpu_custom_call" | custom-call | tf_op jit(solution)/shard_map/project/pallas_call | solution.py:236
  107.5 1.9 slice.33
  109.7 1.8 collective-permute-start.13
  113.5 2.0 collective-permute-done.14.refs_4_
  117.3 6.0 %project_block.3.refs_4_ = f32[512,640]{1,0:T(8,128)S(1)} custom-call(s32[6]{0:T(128)S(1)} %stack.147.index_ref, bf16[1024,512]{1,0:T(8,128)(2,1)} %collective-permute-done.1.refs_0_, bf16[1024,512]{1,0:T(8,128)(2,1)} %copy-done.12, bf16[512,512]{1,0:T(8,128)(2,1)} %collective-permute-done.8.refs_2_, bf16[512,512]{1,0:T(8,128)(2,1)} %collective-permute-done.9.refs_3_, ...), custom_call_target="tpu_custom_call" | custom-call | tf_op jit(solution)/shard_map/project_block/pallas_call | solution.py:326
  124.7 2.5 collective-permute-start.19
  128.8 5.0 %project_block.4 = (bf16[512,512]{1,0:T(8,128)(2,1)S(1)}, bf16[16,16,512]{2,1,0:T(8,128)(2,1)}) custom-call(s32[2]{0:T(128)S(1)} %pad_add_fusion.5.index_ref, bf16[512,512]{1,0:T(8,128)(2,1)} %copy-done.13, bf16[512,512]{1,0:T(8,128)(2,1)} %copy-done.19, bf16[8192,512]{1,0:T(8,128)(2,1)} %bitcast.88, bf16[8192,128]{1,0:T(8,128)(2,1)} %bitcast.93, ...), custom_call_target="tpu_custom_call" | custom-call | tf_op jit(solution)/shard_map/project_block/pallas_call | solution.py:326
  133.8 6.0 %collective-permute-done.19.refs_6_ = bf16[512,512]{1,0:T(8,128)(2,1)S(1)} collective-permute-done((bf16[512,512]{1,0:T(8,128)(2,1)}, bf16[512,512]{1,0:T(8,128)(2,1)S(1)}, u32[]{:S(2)}, u32[]{:S(2)}) %collective-permute-start.19) | collective-permute-done | bytes 524320 | tf_op jit(solution)/shard_map/ppermute | solution.py:59
  140.8 5.3 %all-to-all-start.2 = ((bf16[16,16,512]{2,1,0:T(8,128)(2,1)}), bf16[16,16,512]{2,1,0:T(8,128)(2,1)S(1)}, u32[]{:S(2)}, u32[]{:S(2)}) async-start(bf16[16,16,512]{2,1,0:T(8,128)(2,1)} %get-tuple-element.82), calls=%async_computation.2 | async-start | bytes 524288 | tf_op jit(solution)/shard_map/all_to_all | solution.py:559
  148.0 8.7 %project_block.5 = (bf16[512,512]{1,0:T(8,128)(2,1)S(1)}, bf16[16,16,512]{2,1,0:T(8,128)(2,1)}) custom-call(s32[8]{0:T(128)S(1)} %stack.143.index_ref, bf16[1024,512]{1,0:T(8,128)(2,1)} %collective-permute-done.1.refs_0_, bf16[1024,512]{1,0:T(8,128)(2,1)} %copy-done.12, bf16[512,512]{1,0:T(8,128)(2,1)} %collective-permute-done.10.refs_2_, ...), custom_call_target="tpu_custom_call" | custom-call | tf_op jit(solution)/shard_map/project_block/pallas_call | solution.py:326
  157.5 2.6 attend.2.heads_ref
  160.1 2.8 %chunks.16 = (bf16[1,512,512]{2,1,0:T(8,128)(2,1)S(1)}, bf16[1,512,512]{2,1,0:T(8,128)(2,1)S(1)}) custom-call(s32[2]{0:T(128)S(1)} %pad_add_fusion.4.index_ref, bf16[512,512]{1,0:T(8,128)(2,1)S(1)} %attend.2.heads_ref, bf16[512,8192]{1,0:T(8,128)(2,1)} %bitcast.69), custom_call_target="tpu_custom_call" | custom-call | tf_op jit(solution)/shard_map/chunks/pallas_call | solution.py:458
  163.6 7.2 %all-to-all-start.3 = ((bf16[16,16,512]{2,1,0:T(8,128)(2,1)}), bf16[16,16,512]{2,1,0:T(8,128)(2,1)S(1)}, u32[]{:S(2)}, u32[]{:S(2)}) async-start(bf16[16,16,512]{2,1,0:T(8,128)(2,1)} %get-tuple-element.89), calls=%async_computation.3 | async-start | bytes 524288 | tf_op jit(solution)/shard_map/all_to_all | solution.py:559
  170.9 2.9 %chunks.17 = bf16[2,512,512]{2,1,0:T(8,128)(2,1)S(1)} custom-call(s32[2]{0:T(128)S(1)} %pad_add_fusion.3.index_ref, bf16[512,512]{1,0:T(8,128)(2,1)S(1)} %attend.2.heads_ref, bf16[512,8192]{1,0:T(8,128)(2,1)} %bitcast.70, bf16[1,512,512]{2,1,0:T(8,128)(2,1)S(1)} %collective-permute-done.21.refs_0_, bf16[1,512,512]{2,1,0:T(8,128)(2,1)S(1)} %collective-permute-done.22.refs_1_), custom_call_target="tpu_custom_call" | custom-call | tf_op jit(solution)/shard_map/chunks/pallas_call | solution.py:458
  173.8 2.7 collective-permute-start.26
  176.5 3.0 %all-to-all-done.3 = bf16[16,16,512]{2,1,0:T(8,128)(2,1)S(1)} async-done(((bf16[16,16,512]{2,1,0:T(8,128)(2,1)}), bf16[16,16,512]{2,1,0:T(8,128)(2,1)S(1)}, u32[]{:S(2)}, u32[]{:S(2)}) %all-to-all-start.3) | async-done | bytes 262176 | tf_op jit(solution)/shard_map/all_to_all | solution.py:559
  180.5 3.1 %attend.3.heads_ref = bf16[512,512]{1,0:T(8,128)(2,1)S(1)} custom-call(s32[3,8]{1,0:T(4,128)S(1)} %pad_add_fusion.plan_ref, bf16[512,512]{1,0:T(8,128)(2,1)S(1)} %copy-done.11, bf16[256,512]{1,0:T(8,128)(2,1)S(1)} %bitcast.65, bf16[256,512]{1,0:T(8,128)(2,1)S(1)} %bitcast.68), custom_call_target="tpu_custom_call" | custom-call | tf_op jit(solution)/shard_map/attend/pallas_call | solution.py:389
  183.6 2.9 %chunks.18 = (bf16[1,512,512]{2,1,0:T(8,128)(2,1)S(1)}, bf16[1,512,512]{2,1,0:T(8,128)(2,1)S(1)}) custom-call(s32[2]{0:T(128)S(1)} %pad_add_fusion.4.index_ref, bf16[512,512]{1,0:T(8,128)(2,1)S(1)} %attend.3.heads_ref, bf16[512,8192]{1,0:T(8,128)(2,1)} %bitcast.71), custom_call_target="tpu_custom_call" | custom-call | tf_op jit(solution)/shard_map/chunks/pallas_call | solution.py:458
  190.0 2.9 %chunks.19 = bf16[2,512,512]{2,1,0:T(8,128)(2,1)S(1)} custom-call(s32[2]{0:T(128)S(1)} %pad_add_fusion.3.index_ref, bf16[512,512]{1,0:T(8,128)(2,1)S(1)} %attend.3.heads_ref, bf16[512,8192]{1,0:T(8,128)(2,1)} %bitcast.72, bf16[1,512,512]{2,1,0:T(8,128)(2,1)S(1)} %collective-permute-done.23.refs_0_, bf16[1,512,512]{2,1,0:T(8,128)(2,1)S(1)} %collective-permute-done.24.refs_1_), custom_call_target="tpu_custom_call" | custom-call | tf_op jit(solution)/shard_map/chunks/pallas_call | solution.py:458
  194.0 4.1 %chunks.20 = (bf16[1,512,512]{2,1,0:T(8,128)(2,1)S(1)}, bf16[1,512,512]{2,1,0:T(8,128)(2,1)S(1)}, bf16[1,512,512]{2,1,0:T(8,128)(2,1)S(1)}, bf16[1,512,512]{2,1,0:T(8,128)(2,1)S(1)}) custom-call(s32[4]{0:T(128)S(1)} %pad_add_fusion.2.index_ref, bf16[512,512]{1,0:T(8,128)(2,1)S(1)} %attend.2.heads_ref, bf16[512,8192]{1,0:T(8,128)(2,1)} %bitcast.73), custom_call_target="tpu_custom_call" | custom-call | tf_op jit(solution)/shard_map/chunks/pallas_call | solution.py:458
  202.3 4.3 %chunks.21 = (bf16[2,512,512]{2,1,0:T(8,128)(2,1)S(1)}, bf16[2,512,512]{2,1,0:T(8,128)(2,1)S(1)}) custom-call(s32[4]{0:T(128)S(1)} %pad_add_fusion.1.index_ref, bf16[512,512]{1,0:T(8,128)(2,1)S(1)} %attend.2.heads_ref, bf16[512,8192]{1,0:T(8,128)(2,1)} %bitcast.74, bf16[1,512,512]{2,1,0:T(8,128)(2,1)S(1)} %collective-permute-done.25.refs_0_, ...), custom_call_target="tpu_custom_call" | custom-call | tf_op jit(solution)/shard_map/chunks/pallas_call | solution.py:458
  206.6 2.2 collective-permute-start.35
  208.8 4.1 %chunks.22 = (bf16[1,512,512]{2,1,0:T(8,128)(2,1)S(1)}, bf16[1,512,512]{2,1,0:T(8,128)(2,1)S(1)}, bf16[1,512,512]{2,1,0:T(8,128)(2,1)S(1)}, bf16[1,512,512]{2,1,0:T(8,128)(2,1)S(1)}) custom-call(s32[4]{0:T(128)S(1)} %pad_add_fusion.2.index_ref, bf16[512,512]{1,0:T(8,128)(2,1)S(1)} %attend.3.heads_ref, bf16[512,8192]{1,0:T(8,128)(2,1)} %bitcast.75), custom_call_target="tpu_custom_call" | custom-call | tf_op jit(solution)/shard_map/chunks/pallas_call | solution.py:458
  217.1 4.3 %chunks.23 = (bf16[2,512,512]{2,1,0:T(8,128)(2,1)S(1)}, bf16[2,512,512]{2,1,0:T(8,128)(2,1)S(1)}) custom-call(s32[4]{0:T(128)S(1)} %pad_add_fusion.1.index_ref, bf16[512,512]{1,0:T(8,128)(2,1)S(1)} %attend.3.heads_ref, bf16[512,8192]{1,0:T(8,128)(2,1)} %bitcast.76, bf16[1,512,512]{2,1,0:T(8,128)(2,1)S(1)} %collective-permute-done.30.refs_0_, ...), custom_call_target="tpu_custom_call" | custom-call | tf_op jit(solution)/shard_map/chunks/pallas_call | solution.py:458
  224.6 1.8 collective-permute-start.40
  228.5 6.9 %collective-permute-done.37.refs_0_ = bf16[2,512,512]{2,1,0:T(8,128)(2,1)S(1)} collective-permute-done((bf16[2,512,512]{2,1,0:T(8,128)(2,1)S(1)}, bf16[2,512,512]{2,1,0:T(8,128)(2,1)S(1)}, u32[]{:S(2)}, u32[]{:S(2)}) %collective-permute-start.37) | collective-permute-done | bytes 1048608 | tf_op jit(solution)/shard_map/ppermute | solution.py:59
  237.1 2.3 collective-permute-start.39
  239.4 3.6 %collective-permute-done.38.refs_2_ = bf16[1,512,512]{2,1,0:T(8,128)(2,1)S(1)} collective-permute-done((bf16[1,512,512]{2,1,0:T(8,128)(2,1)S(1)}, bf16[1,512,512]{2,1,0:T(8,128)(2,1)S(1)}, u32[]{:S(2)}, u32[]{:S(2)}) %collective-permute-start.38) | collective-permute-done | bytes 524320 | tf_op jit(solution)/shard_map/ppermute | solution.py:59
  244.7 1.9 collective-permute-done.40.refs_0_
  248.3 2.3 collective-permute-start.41
  252.1 2.5 chunks.29.refs_3_
  254.6 3.2 %collective-permute-done.42.refs_0_ = bf16[2,512,512]{2,1,0:T(8,128)(2,1)S(1)} collective-permute-done((bf16[2,512,512]{2,1,0:T(8,128)(2,1)S(1)}, bf16[2,512,512]{2,1,0:T(8,128)(2,1)S(1)}, u32[]{:S(2)}, u32[]{:S(2)}) %collective-permute-start.42) | collective-permute-done | bytes 1048608 | tf_op jit(solution)/shard_map/ppermute | solution.py:59
  259.6 2.3 collective-permute-start.43
  261.8 3.7 %collective-permute-done.44.refs_2_ = bf16[1,512,512]{2,1,0:T(8,128)(2,1)S(1)} collective-permute-done((bf16[1,512,512]{2,1,0:T(8,128)(2,1)S(1)}, bf16[1,512,512]{2,1,0:T(8,128)(2,1)S(1)}, u32[]{:S(2)}, u32[]{:S(2)}) %collective-permute-start.44) | collective-permute-done | bytes 524320 | tf_op jit(solution)/shard_map/ppermute | solution.py:59
  265.6 2.5 chunks.31
  (148 shorter events, 61.2 us)
Async XLA Ops:
  3.0 11.7 %all-to-all-start = ((s32[8,1,2]{2,1,0:T(1,128)}), s32[8,1,2]{2,1,0:T(1,128)S(1)}, u32[]{:S(2)}, u32[]{:S(2)}) async-start(s32[8,1,2]{2,1,0:T(1,128)} %copy.10), calls=%async_computation | async-start | bytes 8192 | tf_op jit(solution)/shard_map/all_to_all | solution.py:521
  14.7 30.5 %all-to-all-start.1 = ((bf16[8,272,512]{2,1,0:T(8,128)(2,1)}), bf16[8,272,512]{2,1,0:T(8,128)(2,1)S(1)}, u32[]{:S(2)}, u32[]{:S(2)}) async-start(bf16[8,272,512]{2,1,0:T(8,128)(2,1)} %cut.1), calls=%async_computation.1 | async-start | bytes 4456448 | tf_op jit(solution)/shard_map/all_to_all | solution.py:520
  49.3 8.1 %collective-permute-start.3 = (bf16[1024,512]{1,0:T(8,128)(2,1)S(1)}, bf16[1024,512]{1,0:T(8,128)(2,1)}, u32[]{:S(2)}, u32[]{:S(2)}) collective-permute-start(bf16[1024,512]{1,0:T(8,128)(2,1)S(1)} %pack.1), channel_id=1, source_target_pairs={{0,1},{1,0},{2,3},{3,2},{4,5},{5,4},{6,7},{7,6},{8,9},{9,8},{10,11... | collective-permute-start | bytes 3145736 | tf_op jit(solution)/shard_map/ppermute | solution.py:59
  52.1 14.5 %collective-permute-start = (bf16[1024,512]{1,0:T(8,128)(2,1)S(1)}, bf16[1024,512]{1,0:T(8,128)(2,1)S(1)}, u32[]{:S(2)}, u32[]{:S(2)}) collective-permute-start(bf16[1024,512]{1,0:T(8,128)(2,1)S(1)} %pack.1), channel_id=1, source_target_pairs={{0,2},{1,7},{2,4},{3,1},{4,6},{5,3},{6,0},{7,5},{8,10},{9,15},{10,... | collective-permute-start | bytes 3145736 | tf_op jit(solution)/shard_map/ppermute | solution.py:59
  54.9 25.8 %collective-permute-start.2 = (bf16[1024,512]{1,0:T(8,128)(2,1)S(1)}, bf16[1024,512]{1,0:T(8,128)(2,1)S(1)}, u32[]{:S(2)}, u32[]{:S(2)}) collective-permute-start(bf16[1024,512]{1,0:T(8,128)(2,1)S(1)} %pack.1), channel_id=1, source_target_pairs={{0,8},{1,9},{2,10},{3,11},{4,12},{5,13},{6,14},{7,15},{8,0},{9,1},... | collective-permute-start | bytes 3145736 | tf_op jit(solution)/shard_map/ppermute | solution.py:59
  57.4 23.3 %collective-permute-start.4 = (bf16[1024,512]{1,0:T(8,128)(2,1)}, bf16[1024,512]{1,0:T(8,128)(2,1)S(1)}, u32[]{:S(2)}, u32[]{:S(2)}) collective-permute-start(bf16[1024,512]{1,0:T(8,128)(2,1)} %collective-permute-done.3), channel_id=1, source_target_pairs={{0,2},{1,7},{2,4},{3,1},{4,6},{5,3},{6,0},{7,5},{8,10},{9,15},{10,... | collective-permute-start | bytes 3145736 | tf_op jit(solution)/shard_map/ppermute | solution.py:59
  80.7 7.2 %collective-permute-start.7 = (bf16[1024,512]{1,0:T(8,128)(2,1)S(1)}, bf16[1024,512]{1,0:T(8,128)(2,1)S(1)}, u32[]{:S(2)}, u32[]{:S(2)}) collective-permute-start(bf16[1024,512]{1,0:T(8,128)(2,1)S(1)} %collective-permute-done.2), channel_id=1, source_target_pairs={{0,1},{1,0},{2,3},{3,2},{4,5},{5,4},{6,7},{7,6},{8,9},{9,8},{10,11... | collective-permute-start | bytes 3145736 | tf_op jit(solution)/shard_map/ppermute | solution.py:59
  80.9 8.5 %collective-permute-start.5 = (bf16[1024,512]{1,0:T(8,128)(2,1)S(1)}, bf16[1024,512]{1,0:T(8,128)(2,1)S(1)}, u32[]{:S(2)}, u32[]{:S(2)}) collective-permute-start(bf16[1024,512]{1,0:T(8,128)(2,1)S(1)} %collective-permute-done), channel_id=1, source_target_pairs={{0,1},{1,0},{2,3},{3,2},{4,5},{5,4},{6,7},{7,6},{8,9},{9,8},{10,11... | collective-permute-start | bytes 3145736 | tf_op jit(solution)/shard_map/ppermute | solution.py:59
  81.2 9.3 %collective-permute-start.6 = (bf16[1024,512]{1,0:T(8,128)(2,1)S(1)}, bf16[1024,512]{1,0:T(8,128)(2,1)S(1)}, u32[]{:S(2)}, u32[]{:S(2)}) collective-permute-start(bf16[1024,512]{1,0:T(8,128)(2,1)S(1)} %collective-permute-done.4), channel_id=1, source_target_pairs={{0,1},{1,0},{2,3},{3,2},{4,5},{5,4},{6,7},{7,6},{8,9},{9,8},{10,11... | collective-permute-start | bytes 3145736 | tf_op jit(solution)/shard_map/ppermute | solution.py:59
  81.4 26.2 %collective-permute-start.1 = (bf16[1024,512]{1,0:T(8,128)(2,1)S(1)}, bf16[1024,512]{1,0:T(8,128)(2,1)}, u32[]{:S(2)}, u32[]{:S(2)}) collective-permute-start(bf16[1024,512]{1,0:T(8,128)(2,1)S(1)} %collective-permute-done), channel_id=1, source_target_pairs={{0,2},{1,7},{2,4},{3,1},{4,6},{5,3},{6,0},{7,5},{8,10},{9,15},{10,... | collective-permute-start | bytes 3145736 | tf_op jit(solution)/shard_map/ppermute | solution.py:59
  83.8 25.6 %collective-permute-start.10 = (bf16[512,512]{1,0:T(8,128)(2,1)}, bf16[512,512]{1,0:T(8,128)(2,1)}, u32[]{:S(2)}, u32[]{:S(2)}) collective-permute-start(bf16[512,512]{1,0:T(8,128)(2,1)} %slice.39), channel_id=1, source_target_pairs={{0,8},{1,9},{2,10},{3,11},{4,12},{5,13},{6,14},{7,15},{8,0},{9,1},... | collective-permute-start | bytes 1572872 | tf_op jit(solution)/shard_map/ppermute | solution.py:59
  88.0 21.8 %collective-permute-start.11 = (bf16[512,512]{1,0:T(8,128)(2,1)}, bf16[512,512]{1,0:T(8,128)(2,1)}, u32[]{:S(2)}, u32[]{:S(2)}) collective-permute-start(bf16[512,512]{1,0:T(8,128)(2,1)} %slice.37), channel_id=1, source_target_pairs={{0,8},{1,9},{2,10},{3,11},{4,12},{5,13},{6,14},{7,15},{8,0},{9,1},... | collective-permute-start | bytes 1572872 | tf_op jit(solution)/shard_map/ppermute | solution.py:59
  90.3 19.4 %collective-permute-start.8 = (bf16[512,512]{1,0:T(8,128)(2,1)}, bf16[512,512]{1,0:T(8,128)(2,1)}, u32[]{:S(2)}, u32[]{:S(2)}) collective-permute-start(bf16[512,512]{1,0:T(8,128)(2,1)} %slice.34), channel_id=1, source_target_pairs={{0,2},{1,7},{2,4},{3,1},{4,6},{5,3},{6,0},{7,5},{8,10},{9,15},{10,... | collective-permute-start | bytes 1572872 | tf_op jit(solution)/shard_map/ppermute | solution.py:59
  91.5 18.2 %collective-permute-start.9 = (bf16[512,512]{1,0:T(8,128)(2,1)}, bf16[512,512]{1,0:T(8,128)(2,1)}, u32[]{:S(2)}, u32[]{:S(2)}) collective-permute-start(bf16[512,512]{1,0:T(8,128)(2,1)} %slice.38), channel_id=1, source_target_pairs={{0,2},{1,7},{2,4},{3,1},{4,6},{5,3},{6,0},{7,5},{8,10},{9,15},{10,... | collective-permute-start | bytes 1572872 | tf_op jit(solution)/shard_map/ppermute | solution.py:59
  109.7 5.9 %collective-permute-start.13 = (bf16[1024,512]{1,0:T(8,128)(2,1)}, bf16[1024,512]{1,0:T(8,128)(2,1)S(1)}, u32[]{:S(2)}, u32[]{:S(2)}) collective-permute-start(bf16[1024,512]{1,0:T(8,128)(2,1)} %collective-permute-done.1.refs_0_), channel_id=1, source_target_pairs={{0,1},{1,0},{2,3},{3,2},{4,5},{5,4},{6,7},{7,6},{8,9},{9,8},{10,11... | collective-permute-start | bytes 3145736 | tf_op jit(solution)/shard_map/ppermute | solution.py:59
  111.5 4.0 %collective-permute-start.14 = (bf16[512,512]{1,0:T(8,128)(2,1)}, bf16[512,512]{1,0:T(8,128)(2,1)S(1)}, u32[]{:S(2)}, u32[]{:S(2)}) collective-permute-start(bf16[512,512]{1,0:T(8,128)(2,1)} %collective-permute-done.8.refs_2_), channel_id=1, source_target_pairs={{0,1},{1,0},{2,3},{3,2},{4,5},{5,4},{6,7},{7,6},{8,9},{9,8},{10,11... | collective-permute-start | bytes 1572872 | tf_op jit(solution)/shard_map/ppermute | solution.py:59
  111.6 4.0 %collective-permute-start.15 = (bf16[512,512]{1,0:T(8,128)(2,1)}, bf16[512,512]{1,0:T(8,128)(2,1)}, u32[]{:S(2)}, u32[]{:S(2)}) collective-permute-start(bf16[512,512]{1,0:T(8,128)(2,1)} %collective-permute-done.9.refs_3_), channel_id=1, source_target_pairs={{0,1},{1,0},{2,3},{3,2},{4,5},{5,4},{6,7},{7,6},{8,9},{9,8},{10,11... | collective-permute-start | bytes 1572872 | tf_op jit(solution)/shard_map/ppermute | solution.py:59
  112.0 12.3 %collective-permute-start.12 = (bf16[512,512]{1,0:T(8,128)(2,1)}, bf16[512,512]{1,0:T(8,128)(2,1)S(1)}, u32[]{:S(2)}, u32[]{:S(2)}) collective-permute-start(bf16[512,512]{1,0:T(8,128)(2,1)} %collective-permute-done.8.refs_2_), channel_id=1, source_target_pairs={{0,2},{1,7},{2,4},{3,1},{4,6},{5,3},{6,0},{7,5},{8,10},{9,15},{10,... | collective-permute-start | bytes 1572872 | tf_op jit(solution)/shard_map/ppermute | solution.py:59
  124.3 3.6 %collective-permute-start.16 = (bf16[512,512]{1,0:T(8,128)(2,1)S(1)}, bf16[512,512]{1,0:T(8,128)(2,1)S(1)}, u32[]{:S(2)}, u32[]{:S(2)}) collective-permute-start(bf16[512,512]{1,0:T(8,128)(2,1)S(1)} %collective-permute-done.12.refs_0_), channel_id=1, source_target_pairs={{0,1},{1,0},{2,3},{3,2},{4,5},{5,4},{6,7},{7,6},{8,9},{9,8},{10,11... | collective-permute-start | bytes 1572872 | tf_op jit(solution)/shard_map/ppermute | solution.py:59
  124.7 15.1 %collective-permute-start.19 = (bf16[512,512]{1,0:T(8,128)(2,1)}, bf16[512,512]{1,0:T(8,128)(2,1)S(1)}, u32[]{:S(2)}, u32[]{:S(2)}) collective-permute-start(bf16[512,512]{1,0:T(8,128)(2,1)} %slice.33), channel_id=1, source_target_pairs={{0,8},{1,9},{2,10},{3,11},{4,12},{5,13},{6,14},{7,15},{8,0},{9,1},... | collective-permute-start | bytes 1572872 | tf_op jit(solution)/shard_map/ppermute | solution.py:59
  127.3 18.9 %collective-permute-start.17 = (bf16[512,512]{1,0:T(8,128)(2,1)}, bf16[512,512]{1,0:T(8,128)(2,1)S(1)}, u32[]{:S(2)}, u32[]{:S(2)}) collective-permute-start(bf16[512,512]{1,0:T(8,128)(2,1)} %collective-permute-done.10.refs_2_), channel_id=1, source_target_pairs={{0,1},{1,0},{2,3},{3,2},{4,5},{5,4},{6,7},{7,6},{8,9},{9,8},{10,11... | collective-permute-start | bytes 1572872 | tf_op jit(solution)/shard_map/ppermute | solution.py:59
  127.7 18.5 %collective-permute-start.18 = (bf16[512,512]{1,0:T(8,128)(2,1)}, bf16[512,512]{1,0:T(8,128)(2,1)S(1)}, u32[]{:S(2)}, u32[]{:S(2)}) collective-permute-start(bf16[512,512]{1,0:T(8,128)(2,1)} %collective-permute-done.11.refs_3_), channel_id=1, source_target_pairs={{0,1},{1,0},{2,3},{3,2},{4,5},{5,4},{6,7},{7,6},{8,9},{9,8},{10,11... | collective-permute-start | bytes 1572872 | tf_op jit(solution)/shard_map/ppermute | solution.py:59
  139.8 6.4 %collective-permute-start.20 = (bf16[512,512]{1,0:T(8,128)(2,1)S(1)}, bf16[512,512]{1,0:T(8,128)(2,1)S(1)}, u32[]{:S(2)}, u32[]{:S(2)}) collective-permute-start(bf16[512,512]{1,0:T(8,128)(2,1)S(1)} %collective-permute-done.19.refs_6_), channel_id=1, source_target_pairs={{0,1},{1,0},{2,3},{3,2},{4,5},{5,4},{6,7},{7,6},{8,9},{9,8},{10,11... | collective-permute-start | bytes 1572872 | tf_op jit(solution)/shard_map/ppermute | solution.py:59
  140.8 16.7 %all-to-all-start.2 = ((bf16[16,16,512]{2,1,0:T(8,128)(2,1)}), bf16[16,16,512]{2,1,0:T(8,128)(2,1)S(1)}, u32[]{:S(2)}, u32[]{:S(2)}) async-start(bf16[16,16,512]{2,1,0:T(8,128)(2,1)} %get-tuple-element.82), calls=%async_computation.2 | async-start | bytes 524288 | tf_op jit(solution)/shard_map/all_to_all | solution.py:559
  163.0 7.9 %collective-permute-start.21 = (bf16[1,512,512]{2,1,0:T(8,128)(2,1)S(1)}, bf16[1,512,512]{2,1,0:T(8,128)(2,1)S(1)}, u32[]{:S(2)}, u32[]{:S(2)}) collective-permute-start(bf16[1,512,512]{2,1,0:T(8,128)(2,1)S(1)} %get-tuple-element.84), channel_id=1, source_target_pairs={{0,1},{1,0},{2,3},{3,2},{4,5},{5,4},{6,7},{7,6},{8,9},{9,8},{10,11... | collective-permute-start | bytes 1572872 | tf_op jit(solution)/shard_map/ppermute | solution.py:59
  163.2 7.7 %collective-permute-start.22 = (bf16[1,512,512]{2,1,0:T(8,128)(2,1)S(1)}, bf16[1,512,512]{2,1,0:T(8,128)(2,1)S(1)}, u32[]{:S(2)}, u32[]{:S(2)}) collective-permute-start(bf16[1,512,512]{2,1,0:T(8,128)(2,1)S(1)} %get-tuple-element.86), channel_id=1, source_target_pairs={{0,1},{1,0},{2,3},{3,2},{4,5},{5,4},{6,7},{7,6},{8,9},{9,8},{10,11... | collective-permute-start | bytes 1572872 | tf_op jit(solution)/shard_map/ppermute | solution.py:59
  163.6 15.9 %all-to-all-start.3 = ((bf16[16,16,512]{2,1,0:T(8,128)(2,1)}), bf16[16,16,512]{2,1,0:T(8,128)(2,1)S(1)}, u32[]{:S(2)}, u32[]{:S(2)}) async-start(bf16[16,16,512]{2,1,0:T(8,128)(2,1)} %get-tuple-element.89), calls=%async_computation.3 | async-start | bytes 524288 | tf_op jit(solution)/shard_map/all_to_all | solution.py:559
  173.8 24.9 %collective-permute-start.26 = (bf16[2,512,512]{2,1,0:T(8,128)(2,1)S(1)}, bf16[2,512,512]{2,1,0:T(8,128)(2,1)S(1)}, u32[]{:S(2)}, u32[]{:S(2)}) collective-permute-start(bf16[2,512,512]{2,1,0:T(8,128)(2,1)S(1)} %chunks.17), channel_id=1, source_target_pairs={{0,2},{1,7},{2,4},{3,1},{4,6},{5,3},{6,0},{7,5},{8,10},{9,15},{10,... | collective-permute-start | bytes 3145736 | tf_op jit(solution)/shard_map/ppermute | solution.py:59
  186.4 2.8 %collective-permute-start.23 = (bf16[1,512,512]{2,1,0:T(8,128)(2,1)S(1)}, bf16[1,512,512]{2,1,0:T(8,128)(2,1)S(1)}, u32[]{:S(2)}, u32[]{:S(2)}) collective-permute-start(bf16[1,512,512]{2,1,0:T(8,128)(2,1)S(1)} %get-tuple-element.91), channel_id=1, source_target_pairs={{0,1},{1,0},{2,3},{3,2},{4,5},{5,4},{6,7},{7,6},{8,9},{9,8},{10,11... | collective-permute-start | bytes 1572872 | tf_op jit(solution)/shard_map/ppermute | solution.py:59
  187.7 2.3 collective-permute-start.24
  193.0 20.6 %collective-permute-start.31 = (bf16[2,512,512]{2,1,0:T(8,128)(2,1)S(1)}, bf16[2,512,512]{2,1,0:T(8,128)(2,1)S(1)}, u32[]{:S(2)}, u32[]{:S(2)}) collective-permute-start(bf16[2,512,512]{2,1,0:T(8,128)(2,1)S(1)} %chunks.19), channel_id=1, source_target_pairs={{0,2},{1,7},{2,4},{3,1},{4,6},{5,3},{6,0},{7,5},{8,10},{9,15},{10,... | collective-permute-start | bytes 3145736 | tf_op jit(solution)/shard_map/ppermute | solution.py:59
  198.1 2.0 collective-permute-start.25
  198.1 2.6 collective-permute-start.27
  198.6 2.9 %collective-permute-start.28 = (bf16[1,512,512]{2,1,0:T(8,128)(2,1)S(1)}, bf16[1,512,512]{2,1,0:T(8,128)(2,1)S(1)}, u32[]{:S(2)}, u32[]{:S(2)}) collective-permute-start(bf16[1,512,512]{2,1,0:T(8,128)(2,1)S(1)} %get-tuple-element.98), channel_id=1, source_target_pairs={{0,1},{1,0},{2,3},{3,2},{4,5},{5,4},{6,7},{7,6},{8,9},{9,8},{10,11... | collective-permute-start | bytes 1572872 | tf_op jit(solution)/shard_map/ppermute | solution.py:59
  198.7 3.6 %collective-permute-start.29 = (bf16[1,512,512]{2,1,0:T(8,128)(2,1)S(1)}, bf16[1,512,512]{2,1,0:T(8,128)(2,1)S(1)}, u32[]{:S(2)}, u32[]{:S(2)}) collective-permute-start(bf16[1,512,512]{2,1,0:T(8,128)(2,1)S(1)} %get-tuple-element.99), channel_id=1, source_target_pairs={{0,1},{1,0},{2,3},{3,2},{4,5},{5,4},{6,7},{7,6},{8,9},{9,8},{10,11... | collective-permute-start | bytes 1572872 | tf_op jit(solution)/shard_map/ppermute | solution.py:59
  206.6 15.5 %collective-permute-start.35 = (bf16[2,512,512]{2,1,0:T(8,128)(2,1)S(1)}, bf16[2,512,512]{2,1,0:T(8,128)(2,1)S(1)}, u32[]{:S(2)}, u32[]{:S(2)}) collective-permute-start(bf16[2,512,512]{2,1,0:T(8,128)(2,1)S(1)} %get-tuple-element.100), channel_id=1, source_target_pairs={{0,2},{1,7},{2,4},{3,1},{4,6},{5,3},{6,0},{7,5},{8,10},{9,15},{10,... | collective-permute-start | bytes 3145736 | tf_op jit(solution)/shard_map/ppermute | solution.py:59
  212.9 2.6 collective-permute-start.32
  213.4 2.9 %collective-permute-start.33 = (bf16[1,512,512]{2,1,0:T(8,128)(2,1)S(1)}, bf16[1,512,512]{2,1,0:T(8,128)(2,1)S(1)}, u32[]{:S(2)}, u32[]{:S(2)}) collective-permute-start(bf16[1,512,512]{2,1,0:T(8,128)(2,1)S(1)} %get-tuple-element.105), channel_id=1, source_target_pairs={{0,1},{1,0},{2,3},{3,2},{4,5},{5,4},{6,7},{7,6},{8,9},{9,8},{10,11... | collective-permute-start | bytes 1572872 | tf_op jit(solution)/shard_map/ppermute | solution.py:59
  213.5 3.6 %collective-permute-start.34 = (bf16[1,512,512]{2,1,0:T(8,128)(2,1)S(1)}, bf16[1,512,512]{2,1,0:T(8,128)(2,1)S(1)}, u32[]{:S(2)}, u32[]{:S(2)}) collective-permute-start(bf16[1,512,512]{2,1,0:T(8,128)(2,1)S(1)} %get-tuple-element.106), channel_id=1, source_target_pairs={{0,1},{1,0},{2,3},{3,2},{4,5},{5,4},{6,7},{7,6},{8,9},{9,8},{10,11... | collective-permute-start | bytes 1572872 | tf_op jit(solution)/shard_map/ppermute | solution.py:59
  221.4 14.0 %collective-permute-start.37 = (bf16[2,512,512]{2,1,0:T(8,128)(2,1)S(1)}, bf16[2,512,512]{2,1,0:T(8,128)(2,1)S(1)}, u32[]{:S(2)}, u32[]{:S(2)}) collective-permute-start(bf16[2,512,512]{2,1,0:T(8,128)(2,1)S(1)} %get-tuple-element.107), channel_id=1, source_target_pairs={{0,2},{1,7},{2,4},{3,1},{4,6},{5,3},{6,0},{7,5},{8,10},{9,15},{10,... | collective-permute-start | bytes 3145736 | tf_op jit(solution)/shard_map/ppermute | solution.py:59
  223.8 2.5 collective-permute-start.36
  224.6 22.1 %collective-permute-start.40 = (bf16[2,512,512]{2,1,0:T(8,128)(2,1)S(1)}, bf16[2,512,512]{2,1,0:T(8,128)(2,1)S(1)}, u32[]{:S(2)}, u32[]{:S(2)}) collective-permute-start(bf16[2,512,512]{2,1,0:T(8,128)(2,1)S(1)} %get-tuple-element.114), channel_id=1, source_target_pairs={{0,2},{1,7},{2,4},{3,1},{4,6},{5,3},{6,0},{7,5},{8,10},{9,15},{10,... | collective-permute-start | bytes 3145736 | tf_op jit(solution)/shard_map/ppermute | solution.py:59
  228.0 15.0 %collective-permute-start.38 = (bf16[1,512,512]{2,1,0:T(8,128)(2,1)S(1)}, bf16[1,512,512]{2,1,0:T(8,128)(2,1)S(1)}, u32[]{:S(2)}, u32[]{:S(2)}) collective-permute-start(bf16[1,512,512]{2,1,0:T(8,128)(2,1)S(1)} %chunks.25), channel_id=1, source_target_pairs={{0,8},{1,9},{2,10},{3,11},{4,12},{5,13},{6,14},{7,15},{8,0},{9,1},... | collective-permute-start | bytes 1572872 | tf_op jit(solution)/shard_map/ppermute | solution.py:59
  237.1 5.9 %collective-permute-start.39 = (bf16[1,512,512]{2,1,0:T(8,128)(2,1)S(1)}, bf16[1,512,512]{2,1,0:T(8,128)(2,1)S(1)}, u32[]{:S(2)}, u32[]{:S(2)}) collective-permute-start(bf16[1,512,512]{2,1,0:T(8,128)(2,1)S(1)} %chunks.26), channel_id=1, source_target_pairs={{0,1},{1,0},{2,3},{3,2},{4,5},{5,4},{6,7},{7,6},{8,9},{9,8},{10,11... | collective-permute-start | bytes 1572872 | tf_op jit(solution)/shard_map/ppermute | solution.py:59
  239.4 18.5 %collective-permute-start.42 = (bf16[2,512,512]{2,1,0:T(8,128)(2,1)S(1)}, bf16[2,512,512]{2,1,0:T(8,128)(2,1)S(1)}, u32[]{:S(2)}, u32[]{:S(2)}) collective-permute-start(bf16[2,512,512]{2,1,0:T(8,128)(2,1)S(1)} %get-tuple-element.117), channel_id=1, source_target_pairs={{0,2},{1,7},{2,4},{3,1},{4,6},{5,3},{6,0},{7,5},{8,10},{9,15},{10,... | collective-permute-start | bytes 3145736 | tf_op jit(solution)/shard_map/ppermute | solution.py:59
  248.3 3.8 %collective-permute-start.41 = (bf16[1,512,512]{2,1,0:T(8,128)(2,1)S(1)}, bf16[1,512,512]{2,1,0:T(8,128)(2,1)S(1)}, u32[]{:S(2)}, u32[]{:S(2)}) collective-permute-start(bf16[1,512,512]{2,1,0:T(8,128)(2,1)S(1)} %chunks.28), channel_id=1, source_target_pairs={{0,1},{1,0},{2,3},{3,2},{4,5},{5,4},{6,7},{7,6},{8,9},{9,8},{10,11... | collective-permute-start | bytes 1572872 | tf_op jit(solution)/shard_map/ppermute | solution.py:59
  250.6 15.0 %collective-permute-start.44 = (bf16[1,512,512]{2,1,0:T(8,128)(2,1)S(1)}, bf16[1,512,512]{2,1,0:T(8,128)(2,1)S(1)}, u32[]{:S(2)}, u32[]{:S(2)}) collective-permute-start(bf16[1,512,512]{2,1,0:T(8,128)(2,1)S(1)} %chunks.27), channel_id=1, source_target_pairs={{0,8},{1,9},{2,10},{3,11},{4,12},{5,13},{6,14},{7,15},{8,0},{9,1},... | collective-permute-start | bytes 1572872 | tf_op jit(solution)/shard_map/ppermute | solution.py:59
  259.6 6.0 %collective-permute-start.43 = (bf16[1,512,512]{2,1,0:T(8,128)(2,1)S(1)}, bf16[1,512,512]{2,1,0:T(8,128)(2,1)S(1)}, u32[]{:S(2)}, u32[]{:S(2)}) collective-permute-start(bf16[1,512,512]{2,1,0:T(8,128)(2,1)S(1)} %chunks.30), channel_id=1, source_target_pairs={{0,1},{1,0},{2,3},{3,2},{4,5},{5,4},{6,7},{7,6},{8,9},{9,8},{10,11... | collective-permute-start | bytes 1572872 | tf_op jit(solution)/shard_map/ppermute | solution.py:59
  (21 other events, 39.8 us)
